TPU v7x, 512 devices: a whole 4x4x16 slice. The times are simulated.
512 devices in a mesh: dp: 16 (over z_hi, y, core), tensor: 32 (over x, z_lo).
Axes of the slice: x: 4, y: 4, z: 16 (z_hi: 2, z_lo: 8; z = z_hi * 8 + z_lo), core: 2. Of those that a mesh axis runs over, the one named last changes fastest.
Arguments:
- tokens: bfloat16 [128, 16, 4096], P(None, 'dp', 'tensor'), may hold values from -6 to 6
- gate_weight: bfloat16 [4096, 14336], P('dp', 'tensor'), may hold values from -0.09375 to 0.09375
- up_weight: bfloat16 [4096, 14336], P('dp', 'tensor'), may hold values from -0.09375 to 0.09375
- down_weight: bfloat16 [14336, 4096], P('tensor', 'dp'), may hold values from -0.046875 to 0.046875
- ia3_scale: float32 [14336], P('tensor'), may hold values from 0.3 to 3
- cotangent: bfloat16 [128, 16, 4096], P(None, 'dp', 'tensor'), may hold values from -4 to 4
Outputs:
- mixed: bfloat16 [128, 16, 4096], P(None, 'dp', 'tensor')
- input_grad: bfloat16 [128, 16, 4096], P(None, 'dp', 'tensor')
- scale_grad: float32 [14336], P('tensor')
All inputs are finite; a program needn't handle non-finite values.
Results may differ from a plain program's by a relative error of at most 0.0049.
Values may be sent and summed in bfloat16 or wider, within the bound.
No kernel may reach another device: no remote copies, remote signals or barrier semaphores. Data moves between devices by JAX's collectives and lax.ppermute only.
A program may use at most 64 MiB of HBM per device.

v0:
```python
import jax
import jax.numpy as jnp
from jax import lax
from jax.sharding import PartitionSpec as P


def reduce_scale(local_grad):
    return lax.psum(local_grad, "dp")


def per_device(tokens, gate_weight, up_weight, down_weight, ia3_scale, cotangent):
    seq_len, seq_local, local_width = tokens.shape
    gathered = lax.all_gather(tokens, "tensor", axis=2, tiled=True)
    model_width = gathered.shape[2]
    token_rows = gathered.reshape(-1, model_width)
    gate_full, up_full = (
        lax.all_gather(gate_weight, "dp", axis=0, tiled=True),
        lax.all_gather(up_weight, "dp", axis=0, tiled=True),
    )
    gate_pre = jnp.dot(token_rows, gate_full, preferred_element_type=jnp.float32)
    up_proj = jnp.dot(token_rows, up_full, preferred_element_type=jnp.float32)
    sigmoid_gate = jax.nn.sigmoid(gate_pre)
    swish_gate = gate_pre * sigmoid_gate
    activated = swish_gate * up_proj
    hidden = (activated * ia3_scale).astype(jnp.bfloat16)
    down_full = lax.all_gather(down_weight, "dp", axis=1, tiled=True)
    mixed = lax.psum_scatter(
        lax.dot_general(
            down_full, hidden, (((0,), (1,)), ((), ())), preferred_element_type=jnp.float32
        ),
        "tensor",
        scatter_dimension=0,
        tiled=True,
    )
    mixed = mixed.T.reshape(seq_len, seq_local, local_width).astype(jnp.bfloat16)
    grad_rows = lax.all_gather(cotangent, "tensor", axis=2, tiled=True).reshape(-1, model_width)
    back = lax.dot_general(
        grad_rows, down_full, (((1,), (1,)), ((), ())), preferred_element_type=jnp.float32
    )
    local_grad = jnp.sum(back * activated, axis=0)
    hidden_grad = back * ia3_scale
    gate_grad = (
        hidden_grad * up_proj * sigmoid_gate * (1.0 + gate_pre * (1.0 - sigmoid_gate))
    ).astype(jnp.bfloat16)
    up_grad = (hidden_grad * swish_gate).astype(jnp.bfloat16)
    first_term = lax.dot_general(
        gate_full, gate_grad, (((1,), (1,)), ((), ())), preferred_element_type=jnp.float32
    )
    second_term = lax.dot_general(
        up_full, up_grad, (((1,), (1,)), ((), ())), preferred_element_type=jnp.float32
    )
    input_grad = lax.psum_scatter(
        first_term + second_term, "tensor", scatter_dimension=0, tiled=True
    )
    input_grad = input_grad.T.reshape(seq_len, seq_local, local_width).astype(jnp.bfloat16)
    scale_grad = reduce_scale(local_grad)
    return (mixed, input_grad, scale_grad)


def solution(mesh):
    in_specs = (
        P(None, "dp", "tensor"),
        P("dp", "tensor"),
        P("dp", "tensor"),
        P("tensor", "dp"),
        P("tensor"),
        P(None, "dp", "tensor"),
    )
    out_specs = (P(None, "dp", "tensor"), P(None, "dp", "tensor"), P("tensor"))
    return jax.shard_map(
        per_device, mesh=mesh, in_specs=in_specs, out_specs=out_specs, check_vma=False
    )
```

profile of v0, /device:TPU:24, one launch (start us, length us, event | category | flops | bytes accessed | tf_op | source)
XLA Modules:
  0.0 1182.8 jit_solution(15286686954979993771)
XLA Ops:
  7.2 0.0 all-gather.6.cloned.1.call-start
  7.2 0.7 all-gather.6.cloned.1.call-update
  7.9 0.0 all-gather.10.cloned.1.call-start
  7.9 0.7 all-gather.10.cloned.1.call-update
  8.6 0.0 all-gather.8.cloned.1.call-start
  8.7 0.7 all-gather.8.cloned.1.call-update
  9.4 0.0 all-gather.12.cloned.1.call-start
  9.4 0.5 all-gather.12.cloned.1.call-update
  10.0 0.0 all-gather.14.cloned.1.call-start
  10.0 0.5 all-gather.14.cloned.1.call-update
  10.5 0.0 reduce-scatter.3.cloned.1.call-start
  10.6 184.8 %all-gather.6.cloned.1.call-done = bf16[128,1,4096]{2,0,1:T(8,128)(2,1)} async-done(((bf16[128,1,128]{2,0,1:T(8,128)(2,1)}), bf16[128,1,4096]{2,0,1:T(8,128)(2,1)}) %all-gather.6.cloned.1.call-update) | async-done | bytes 1048592 | tf_op jit(solution)/shard_map/all_gather | solution.py:13
  195.4 0.0 copy-start.2
  195.4 105.7 %all-gather.10.cloned.1.call-done = bf16[4096,448]{0,1:T(8,128)(2,1)} async-done(((bf16[256,448]{0,1:T(8,128)(2,1)}), bf16[4096,448]{0,1:T(8,128)(2,1)}) %all-gather.10.cloned.1.call-update) | async-done | bytes 3670032 | tf_op jit(solution)/shard_map/all_gather | solution.py:18
  301.1 3.5 fusion.3
  304.6 0.0 copy-start.3
  304.6 104.7 %all-gather.8.cloned.1.call-done = bf16[4096,448]{0,1:T(8,128)(2,1)} async-done(((bf16[256,448]{0,1:T(8,128)(2,1)}), bf16[4096,448]{0,1:T(8,128)(2,1)}) %all-gather.8.cloned.1.call-update) | async-done | bytes 3670032 | tf_op jit(solution)/shard_map/all_gather | solution.py:17
  409.3 0.0 copy-done.2
  409.3 3.2 fusion.5
  412.5 104.9 %all-gather.12.cloned.1.call-done = bf16[448,4096]{1,0:T(8,128)(2,1)} async-done(((bf16[448,256]{1,0:T(8,128)(2,1)}), bf16[448,4096]{1,0:T(8,128)(2,1)}) %all-gather.12.cloned.1.call-update) | async-done | bytes 3670032 | tf_op jit(solution)/shard_map/all_gather | solution.py:26
  517.4 0.0 copy-done.3
  517.4 4.3 convolution_bitcast_fusion
  521.6 0.0 reduce-scatter.3.cloned.1.call-update
  521.7 0.0 reduce-scatter.5.cloned.1.call-start
  521.7 173.1 %all-gather.14.cloned.1.call-done = bf16[128,1,4096]{2,0,1:T(8,128)(2,1)} async-done(((bf16[128,1,128]{2,0,1:T(8,128)(2,1)}), bf16[128,1,4096]{2,0,1:T(8,128)(2,1)}) %all-gather.14.cloned.1.call-update) | async-done | bytes 1048592 | tf_op jit(solution)/shard_map/all_gather | solution.py:36
  694.9 0.0 copy-start.1
  694.9 3.7 multiply_reduce_fusion
  698.6 0.0 copy-start
  698.6 0.0 copy-done.1
  698.6 0.9 fusion.8
  699.5 1.2 copy-done
  700.6 2.2 fusion
  702.8 0.0 reduce-scatter.5.cloned.1.call-update
  702.8 52.8 %psum.7 = f32[448]{0:T(512)} all-reduce(f32[448]{0:T(512)S(1)} %get-tuple-element.3), channel_id=1, replica_groups=mesh['dp'=16,'tensor'=32] {'dp'}, use_global_device_ids=true, to_apply=%region_3.0 | all-reduce | flops 448 | bytes 3584 | tf_op jit(solution)/shard_map/psum | solution.py:8
  755.6 178.9 %reduce-scatter.3.cloned.1.call-done = f32[128,128]{0,1:T(8,128)} async-done(((f32[4096,128]{0,1:T(8,128)}), f32[128,128]{0,1:T(8,128)}) %reduce-scatter.3.cloned.1.call-update) | async-done | bytes 65552 | tf_op jit(solution)/shard_map/reduce_scatter | solution.py:27
  934.6 1.5 convert_bitcast_fusion.1
  936.0 238.5 %reduce-scatter.5.cloned.1.call-done = f32[128,128]{0,1:T(8,128)} async-done(((f32[4096,128]{0,1:T(8,128)}), f32[128,128]{0,1:T(8,128)}) %reduce-scatter.5.cloned.1.call-update) | async-done | bytes 65552 | tf_op jit(solution)/shard_map/reduce_scatter | solution.py:52
  1174.5 1.5 convert_bitcast_fusion
Async XLA Ops:
  7.2 188.2 %all-gather.6.cloned.1.call-start = ((), (), s32[]{:S(2)}) async-start(), calls=%async_computation.2 | async-start | bytes 1081344 | tf_op jit(solution)/shard_map/all_gather | solution.py:13
  7.9 293.2 %all-gather.10.cloned.1.call-start = ((), (), s32[]{:S(2)}) async-start(), calls=%async_computation.4 | async-start | bytes 3899392 | tf_op jit(solution)/shard_map/all_gather | solution.py:18
  8.6 400.7 %all-gather.8.cloned.1.call-start = ((), (), s32[]{:S(2)}) async-start(), calls=%async_computation.3 | async-start | bytes 3899392 | tf_op jit(solution)/shard_map/all_gather | solution.py:17
  9.4 508.0 %all-gather.12.cloned.1.call-start = ((), (), s32[]{:S(2)}) async-start(), calls=%async_computation.5 | async-start | bytes 3899392 | tf_op jit(solution)/shard_map/all_gather | solution.py:26
  10.0 684.9 %all-gather.14.cloned.1.call-start = ((), (), s32[]{:S(2)}) async-start(), calls=%async_computation.7 | async-start | bytes 1081344 | tf_op jit(solution)/shard_map/all_gather | solution.py:36
  10.5 924.0 %reduce-scatter.3.cloned.1.call-start = ((), (), s32[]{:S(2)}) async-start(), calls=%async_computation.6 | async-start | bytes 2162688 | tf_op jit(solution)/shard_map/reduce_scatter | solution.py:27
  195.4 213.9 %copy-start.2 = (bf16[128,1,4096]{2,0,1:T(8,128)(2,1)S(1)}, bf16[128,1,4096]{2,0,1:T(8,128)(2,1)}, u32[]{:S(2)}) copy-start(bf16[128,1,4096]{2,0,1:T(8,128)(2,1)} %all-gather.6.cloned.1.call-done) | copy-start | bytes 3145732
  304.6 212.8 %copy-start.3 = (f32[448]{0:T(512)S(1)}, f32[448]{0:T(512)}, u32[]{:S(2)}) copy-start(f32[448]{0:T(512)} %param.10) | copy-start | bytes 5380
  521.7 652.8 %reduce-scatter.5.cloned.1.call-start = ((), (), s32[]{:S(2)}) async-start(), calls=%async_computation.8 | async-start | bytes 2162688 | tf_op jit(solution)/shard_map/reduce_scatter | solution.py:52
  694.9 3.7 copy-start.1
  698.6 2.0 copy-start
Sparse Core Ops, SparseCore 0:
  10.0 185.3 all-gather.5
  198.5 102.5 all-gather.9
  304.3 105.0 all-gather.7
  412.3 105.0 all-gather.11
  519.2 175.5 all-gather.13
  697.5 236.9 reduce-scatter.2
  937.6 236.8 reduce-scatter.4
where the time goes:
time: 1180 us
  waiting for transfers between devices  1090 us (92%)
  blocking collectives  52.8 us (4%)
  matrix products  17.6 us (1%)
  between operations  14.2 us (1%)
    reduce_scatter x1, waiting for transfers between devices, per_device(): lax.psum_scatter(first_term + second_term, 'tensor', scatter_dimension=0,...  238 us
    all_gather x1, waiting for transfers between devices, per_device(): gathered = lax.all_gather(tokens, 'tensor', axis=2, tiled=True)  185 us
    reduce_scatter x1, waiting for transfers between devices, per_device(): lax.psum_scatter(lax.dot_general(down_full, hidden, (((0,), (1,)), ((), (...  179 us
    all_gather x1, waiting for transfers between devices, per_device(): lax.all_gather(cotangent, 'tensor', axis=2, tiled=True)  173 us
    all_gather x1, waiting for transfers between devices, per_device(): lax.all_gather(up_weight, 'dp', axis=0, tiled=True)  106 us
    all_gather x1, waiting for transfers between devices, per_device(): down_full = lax.all_gather(down_weight, 'dp', axis=1, tiled=True)  105 us
    all_gather x1, waiting for transfers between devices, per_device(): lax.all_gather(gate_weight, 'dp', axis=0, tiled=True)  105 us
    psum x1, blocking collectives, reduce_scale(): return lax.psum(local_grad, 'dp')  52.8 us
  transfers between devices with their start and end apart: 7, of which 7 were waited for; matrix products, arithmetic and copies ran while one was open for 2% of the time, Pallas kernels for 0%

commit v1 on v0

v1 whole, which is shorter than its diff:
```python
import jax
import jax.numpy as jnp
from jax import lax
from jax.sharding import Mesh, PartitionSpec as P

ROWS_AXES = ("zh", "y", "c")
COLS_AXES = ("x", "zl")


def spread(block, axis, size):
    copies = jnp.broadcast_to(block[None], (size,) + block.shape)
    return lax.all_to_all(copies, axis, 0, 0, tiled=True)


def swap(block, axis):
    return lax.ppermute(block, axis, [(0, 1), (1, 0)])


def make_per_device(size):
    nh, ny, nc, nx, nl = (size[a] for a in ("zh", "y", "c", "x", "zl"))

    def per_device(tokens, gate_weight, up_weight, down_weight, ia3_scale, cotangent):
        seq_len, seq_local, width = tokens.shape
        rows = seq_len * seq_local
        model = width * nx * nl
        depth = model // (nh * ny * nc)
        hid = gate_weight.shape[1]
        zh, c = lax.axis_index("zh"), lax.axis_index("c")

        def gather(weight):
            other = swap(weight, "zh")
            first = jnp.where(zh == 0, weight, other)
            second = jnp.where(zh == 0, other, weight)
            column = spread(jnp.stack([first, second]), "y", ny)
            return column, swap(column, "c")

        acts = jnp.stack([tokens.reshape(rows, width), cotangent.reshape(rows, width)])
        acts = spread(acts, "zl", nl)
        acts = spread(acts, "x", nx)
        acts = acts.transpose(2, 3, 0, 1, 4).reshape(2, rows, nh, ny, nc, depth)
        acts = acts.transpose(0, 4, 1, 3, 2, 5).reshape(2, nc, rows, model // nc)
        tok = [lax.dynamic_index_in_dim(acts[0], k, 0, False) for k in (c, 1 - c)]
        cot = [lax.dynamic_index_in_dim(acts[1], k, 0, False) for k in (c, 1 - c)]

        gate = [w.reshape(-1, hid) for w in gather(gate_weight)]
        up = [w.reshape(-1, hid) for w in gather(up_weight)]
        down = [w.reshape(-1, hid) for w in gather(down_weight.T)]

        def times(a, b):
            parts = [jnp.dot(p, q, preferred_element_type=jnp.float32) for p, q in zip(a, b)]
            return parts[0] + parts[1]

        gate_pre = times(tok, gate)
        up_proj = times(tok, up)
        back = times(cot, down)
        sigmoid_gate = jax.nn.sigmoid(gate_pre)
        swish_gate = gate_pre * sigmoid_gate
        activated = swish_gate * up_proj
        hidden = (activated * ia3_scale).astype(jnp.bfloat16)
        local_grad = jnp.sum(back * activated, axis=0)
        hidden_grad = back * ia3_scale
        gate_grad = (
            hidden_grad * up_proj * sigmoid_gate * (1.0 + gate_pre * (1.0 - sigmoid_gate))
        ).astype(jnp.bfloat16)
        up_grad = (hidden_grad * swish_gate).astype(jnp.bfloat16)

        def turned(a, b):
            return lax.dot_general(
                a, b, (((1,), (1,)), ((), ())), preferred_element_type=jnp.float32
            )

        def partial(k):
            mixed = turned(hidden, down[k])
            grad = turned(gate_grad, gate[k]) + turned(up_grad, up[k])
            return jnp.stack([mixed, grad]).astype(jnp.bfloat16)

        own, other = partial(0), partial(1)
        first = jnp.where(c == 0, own, other)
        second = jnp.where(c == 0, other, own)
        outs = jnp.stack([first, second])
        outs = outs.reshape(nc, 2, rows, ny, nh, depth).transpose(4, 3, 0, 5, 1, 2)
        outs = outs.reshape(nx, nl, width, 2, rows).transpose(0, 1, 3, 4, 2)
        outs = lax.all_to_all(outs, "x", 0, 0, tiled=True)
        outs = jnp.sum(outs.astype(jnp.float32), axis=0).astype(jnp.bfloat16)
        outs = lax.all_to_all(outs, "zl", 0, 0, tiled=True)
        outs = jnp.sum(outs.astype(jnp.float32), axis=0).astype(jnp.bfloat16)
        mixed = outs[0].reshape(tokens.shape)
        input_grad = outs[1].reshape(tokens.shape)
        scale_grad = jnp.sum(spread(local_grad, ROWS_AXES, nh * ny * nc), axis=0)
        return mixed, input_grad, scale_grad

    return per_device


def solution(mesh):
    shape = {"zh": 2, "y": 4, "c": 2, "x": 4, "zl": 8}
    fine = Mesh(mesh.devices.reshape(tuple(shape.values())), tuple(shape))
    in_specs = (
        P(None, ROWS_AXES, COLS_AXES),
        P(ROWS_AXES, COLS_AXES),
        P(ROWS_AXES, COLS_AXES),
        P(COLS_AXES, ROWS_AXES),
        P(COLS_AXES),
        P(None, ROWS_AXES, COLS_AXES),
    )
    out_specs = (
        P(None, ROWS_AXES, COLS_AXES),
        P(None, ROWS_AXES, COLS_AXES),
        P(COLS_AXES),
    )
    return jax.shard_map(
        make_per_device(shape),
        mesh=fine,
        in_specs=in_specs,
        out_specs=out_specs,
        check_vma=False,
    )
```

time: 1180 us -> 374 us (0.32)
  waiting for transfers between devices: 1090 us -> 133 us
  starting transfers between devices: 0.27 us -> 107 us
  local copies, waits for them, and re-layouts: 1.19 us -> 82.8 us
  blocking collectives: 52.8 us -> 31.5 us
  between operations: 14.2 us -> 1.01 us
    all_gather x5 -> x0, waiting for transfers between devices: 673 us -> none  [the longest x1 185 us: per_device(): gathered = lax.all_gather(tokens, 'tensor', axis=2, tiled=True)]
    reduce_scatter x2 -> x0, waiting for transfers between devices: 417 us -> none  [the longest x1 238 us: per_device(): lax.psum_scatter(first_term + second_term, 'tensor', scatter_dimension=0,...]
    all_to_all x0 -> x7, waiting for transfers between devices: none -> 103 us  [the longest x6 75 us: spread(): return lax.all_to_all(copies, axis, 0, 0, tiled=True)]
    all_to_all x0 -> x7, starting transfers between devices: none -> 70.2 us  [the longest x6 58.4 us: spread(): return lax.all_to_all(copies, axis, 0, 0, tiled=True)]
    psum x1 -> x0, blocking collectives: 52.8 us -> none  [reduce_scale(): return lax.psum(local_grad, 'dp')]
    ppermute x0 -> x6, starting transfers between devices: none -> 36.5 us  [swap(): return lax.ppermute(block, axis, [(0, 1), (1, 0)])]
    all_to_all x0 -> x1, blocking collectives: none -> 31.5 us  [per_device(): outs = lax.all_to_all(outs, 'x', 0, 0, tiled=True)]
    reshape x0 -> x6, local copies, waits for them, and re-layouts: none -> 30.8 us  [the longest x2 10.6 us: per_device(): down = [w.reshape(-1, hid) for w in gather(down_weight.T)]]
  transfers between devices with their start and end apart: 7 -> 13, of which waited for: 7 -> 9; matrix products, arithmetic and copies ran while one was open for 2% -> 15% of each run, Pallas kernels for 0% -> 0%
where the time goes in v1:
time: 374 us; the launch traced here: 371 us
  waiting for transfers between devices  133 us (36%)
  starting transfers between devices  107 us (29%)
  local copies, waits for them, and re-layouts  82.8 us (22%)
  blocking collectives  31.5 us (8%)
  matrix products  13.5 us (4%)
    all_to_all x6, waiting for transfers between devices, spread(): return lax.all_to_all(copies, axis, 0, 0, tiled=True)  75 us
    all_to_all x6, starting transfers between devices, spread(): return lax.all_to_all(copies, axis, 0, 0, tiled=True)  58.4 us
    ppermute x6, starting transfers between devices, swap(): return lax.ppermute(block, axis, [(0, 1), (1, 0)])  36.5 us
    all_to_all x1, blocking collectives, per_device(): outs = lax.all_to_all(outs, 'x', 0, 0, tiled=True)  31.5 us
    ppermute x6, waiting for transfers between devices, swap(): return lax.ppermute(block, axis, [(0, 1), (1, 0)])  29.2 us
    all_to_all x1, waiting for transfers between devices, per_device(): outs = lax.all_to_all(outs, 'zl', 0, 0, tiled=True)  28.4 us
    all_to_all x5, local copies, waits for them, and re-layouts, spread(): return lax.all_to_all(copies, axis, 0, 0, tiled=True)  15.8 us
    ppermute x3, local copies, waits for them, and re-layouts, swap(): return lax.ppermute(block, axis, [(0, 1), (1, 0)])  13.9 us
  transfers between devices with their start and end apart: 13, of which 9 were waited for; matrix products, arithmetic and copies ran while one was open for 15% of the time, Pallas kernels for 0%

profile of v1, /device:TPU:24, one launch (start us, length us, event | category | flops | bytes accessed | tf_op | source)
XLA Modules:
  0.0 370.9 jit_solution(1767953690714911571)
XLA Ops:
  0.6 15.7 %collective-permute-start.2 = (bf16[256,448]{0,1:T(8,128)(2,1)}, bf16[256,448]{0,1:T(8,128)(2,1)S(1)}, u32[]{:S(2)}, u32[]{:S(2)}) collective-permute-start(bf16[256,448]{0,1:T(8,128)(2,1)} %param.8), channel_id=1, source_target_pairs={{0,256},{256,0},{1,257},{257,1},{2,258},{258,2},{3,259},{259,3},{4... | collective-permute-start | bytes 688136 | tf_op jit(solution)/shard_map/ppermute | solution.py:16
  16.4 1.9 collective-permute-start.4
  18.3 11.6 %collective-permute-done.2 = bf16[256,448]{0,1:T(8,128)(2,1)S(1)} collective-permute-done((bf16[256,448]{0,1:T(8,128)(2,1)}, bf16[256,448]{0,1:T(8,128)(2,1)S(1)}, u32[]{:S(2)}, u32[]{:S(2)}) %collective-permute-start.2) | collective-permute-done | bytes 229408 | tf_op jit(solution)/shard_map/ppermute | solution.py:16
  29.9 12.2 %collective-permute-done.4 = bf16[256,448]{0,1:T(8,128)(2,1)S(1)} collective-permute-done((bf16[256,448]{0,1:T(8,128)(2,1)}, bf16[256,448]{0,1:T(8,128)(2,1)S(1)}, u32[]{:S(2)}, u32[]{:S(2)}) %collective-permute-start.4) | collective-permute-done | bytes 229408 | tf_op jit(solution)/shard_map/ppermute | solution.py:16
  43.3 1.4 broadcast_in_dim.15
  44.6 5.2 %all-to-all-start.3 = ((bf16[4,2,256,448]{2,3,1,0:T(8,128)(2,1)}), bf16[4,2,256,448]{2,3,1,0:T(8,128)(2,1)}, u32[]{:S(2)}, u32[]{:S(2)}) async-start(bf16[4,2,256,448]{2,3,1,0:T(8,128)(2,1)} %broadcast_in_dim.15), calls=%async_computation.3 | async-start | bytes 3670016 | tf_op jit(solution)/shard_map/all_to_all | solution.py:12
  49.9 12.4 %collective-permute-start = (bf16[256,448]{0,1:T(8,128)(2,1)S(1)}, bf16[256,448]{0,1:T(8,128)(2,1)S(1)}, u32[]{:S(2)}, u32[]{:S(2)}) collective-permute-start(bf16[256,448]{0,1:T(8,128)(2,1)S(1)} %copy-done.11), channel_id=1, source_target_pairs={{0,256},{256,0},{1,257},{257,1},{2,258},{258,2},{3,259},{259,3},{4... | collective-permute-start | bytes 688136 | tf_op jit(solution)/shard_map/ppermute | solution.py:16
  62.3 5.3 %collective-permute-done = bf16[256,448]{0,1:T(8,128)(2,1)S(1)} collective-permute-done((bf16[256,448]{0,1:T(8,128)(2,1)S(1)}, bf16[256,448]{0,1:T(8,128)(2,1)S(1)}, u32[]{:S(2)}, u32[]{:S(2)}) %collective-permute-start) | collective-permute-done | bytes 229408 | tf_op jit(solution)/shard_map/ppermute | solution.py:16
  67.7 3.2 all-to-all-done.3
  70.9 1.4 broadcast_in_dim.14
  72.3 6.6 %all-to-all-start.2 = ((bf16[4,2,256,448]{2,3,1,0:T(8,128)(2,1)}), bf16[4,2,256,448]{2,3,1,0:T(8,128)(2,1)}, u32[]{:S(2)}, u32[]{:S(2)}) async-start(bf16[4,2,256,448]{2,3,1,0:T(8,128)(2,1)} %broadcast_in_dim.14), calls=%async_computation.2 | async-start | bytes 3670016 | tf_op jit(solution)/shard_map/all_to_all | solution.py:12
  79.0 20.0 %all-to-all-done.2 = bf16[4,2,256,448]{2,3,1,0:T(8,128)(2,1)} async-done(((bf16[4,2,256,448]{2,3,1,0:T(8,128)(2,1)}), bf16[4,2,256,448]{2,3,1,0:T(8,128)(2,1)}, u32[]{:S(2)}, u32[]{:S(2)}) %all-to-all-start.2) | async-done | bytes 1835040 | tf_op jit(solution)/shard_map/all_to_all | solution.py:12
  99.9 22.5 %all-to-all-start = ((bf16[8,2,128,128]{2,3,1,0:T(8,128)(2,1)}), bf16[8,2,128,128]{2,3,1,0:T(8,128)(2,1)S(1)}, u32[]{:S(2)}, u32[]{:S(2)}) async-start(bf16[8,2,128,128]{2,3,1,0:T(8,128)(2,1)} %broadcast_in_dim.12), calls=%async_computation | async-start | bytes 1048576 | tf_op jit(solution)/shard_map/all_to_all | solution.py:12
  122.4 26.7 %all-to-all-done = bf16[8,2,128,128]{2,3,1,0:T(8,128)(2,1)S(1)} async-done(((bf16[8,2,128,128]{2,3,1,0:T(8,128)(2,1)}), bf16[8,2,128,128]{2,3,1,0:T(8,128)(2,1)S(1)}, u32[]{:S(2)}, u32[]{:S(2)}) %all-to-all-start) | async-done | bytes 524320 | tf_op jit(solution)/shard_map/all_to_all | solution.py:12
  149.1 1.4 broadcast_in_dim.16
  150.5 6.4 %all-to-all-start.4 = ((bf16[4,2,256,448]{2,3,1,0:T(8,128)(2,1)}), bf16[4,2,256,448]{2,3,1,0:T(8,128)(2,1)}, u32[]{:S(2)}, u32[]{:S(2)}) async-start(bf16[4,2,256,448]{2,3,1,0:T(8,128)(2,1)} %broadcast_in_dim.16), calls=%async_computation.4 | async-start | bytes 3670016 | tf_op jit(solution)/shard_map/all_to_all | solution.py:12
  156.9 13.6 %all-to-all-done.4 = bf16[4,2,256,448]{2,3,1,0:T(8,128)(2,1)} async-done(((bf16[4,2,256,448]{2,3,1,0:T(8,128)(2,1)}), bf16[4,2,256,448]{2,3,1,0:T(8,128)(2,1)}, u32[]{:S(2)}, u32[]{:S(2)}) %all-to-all-start.4) | async-done | bytes 1835040 | tf_op jit(solution)/shard_map/all_to_all | solution.py:12
  170.5 1.8 broadcast_in_dim.13
  172.3 4.5 %all-to-all-start.1 = ((bf16[4,8,2,128,128]{3,4,1,2,0:T(8,128)(2,1)}), bf16[4,8,2,128,128]{3,4,1,2,0:T(8,128)(2,1)}, u32[]{:S(2)}, u32[]{:S(2)}) async-start(bf16[4,8,2,128,128]{3,4,1,2,0:T(8,128)(2,1)} %broadcast_in_dim.13), calls=%async_computation.1 | async-start | bytes 4194304 | tf_op jit(solution)/shard_map/all_to_all | solution.py:12
  176.8 1.9 collective-permute-start.3
  178.7 2.4 collective-permute-start.1
  181.1 2.1 collective-permute-start.5
  183.2 4.7 %copy.105 = bf16[4,2,256,448]{2,1,0,3:T(2,128)(2,1)} copy(bf16[4,2,256,448]{2,3,1,0:T(8,128)(2,1)} %all-to-all-done.3) | data formatting | bytes 3670016 | tf_op jit(solution)/shard_map/all_to_all | solution.py:12
  188.0 4.4 %reshape.185 = bf16[2048,448]{0,1:T(8,128)(2,1)S(1)} reshape(bf16[4,2,256,448]{2,1,0,3:T(2,128)(2,1)} %copy.105) | data formatting | bytes 3670016 | tf_op jit(solution)/shard_map/reshape | solution.py:46
  192.4 4.6 %copy.103 = bf16[4,2,256,448]{2,1,0,3:T(2,128)(2,1)} copy(bf16[4,2,256,448]{2,3,1,0:T(8,128)(2,1)} %all-to-all-done.2) | data formatting | bytes 3670016 | tf_op jit(solution)/shard_map/all_to_all | solution.py:12
  197.0 5.3 %reshape.183 = bf16[2048,448]{0,1:T(8,128)(2,1)} reshape(bf16[4,2,256,448]{2,1,0,3:T(2,128)(2,1)} %copy.103) | data formatting | bytes 3670016 | tf_op jit(solution)/shard_map/reshape | solution.py:45
  202.3 4.6 %copy.108 = bf16[4,2,256,448]{2,1,0,3:T(2,128)(2,1)} copy(bf16[4,2,256,448]{2,3,1,0:T(8,128)(2,1)} %all-to-all-done.4) | data formatting | bytes 3670016 | tf_op jit(solution)/shard_map/all_to_all | solution.py:12
  206.9 5.3 %reshape.187 = bf16[2048,448]{0,1:T(8,128)(2,1)} reshape(bf16[4,2,256,448]{2,1,0,3:T(2,128)(2,1)} %copy.108) | data formatting | bytes 3670016 | tf_op jit(solution)/shard_map/reshape | solution.py:47
  212.2 1.7 copy.101
  217.6 1.3 fusion.5
  219.0 4.6 %copy.106 = bf16[4,2,256,448]{2,1,0,3:T(2,128)(2,1)} copy(bf16[4,2,256,448]{2,3,1,0:T(8,128)(2,1)} %collective-permute-done.3) | data formatting | bytes 3670016 | tf_op jit(solution)/shard_map/ppermute | solution.py:16
  223.6 5.3 %reshape.186 = bf16[2048,448]{0,1:T(8,128)(2,1)} reshape(bf16[4,2,256,448]{2,1,0,3:T(2,128)(2,1)} %copy.106) | data formatting | bytes 3670016 | tf_op jit(solution)/shard_map/reshape | solution.py:46
  228.9 4.6 %copy.104 = bf16[4,2,256,448]{2,1,0,3:T(2,128)(2,1)} copy(bf16[4,2,256,448]{2,3,1,0:T(8,128)(2,1)} %collective-permute-done.1) | data formatting | bytes 3670016 | tf_op jit(solution)/shard_map/ppermute | solution.py:16
  233.5 5.3 %reshape.184 = bf16[2048,448]{0,1:T(8,128)(2,1)} reshape(bf16[4,2,256,448]{2,1,0,3:T(2,128)(2,1)} %copy.104) | data formatting | bytes 3670016 | tf_op jit(solution)/shard_map/reshape | solution.py:45
  238.8 4.6 %copy.109 = bf16[4,2,256,448]{2,1,0,3:T(2,128)(2,1)} copy(bf16[4,2,256,448]{2,3,1,0:T(8,128)(2,1)} %collective-permute-done.5) | data formatting | bytes 3670016 | tf_op jit(solution)/shard_map/ppermute | solution.py:16
  243.4 5.3 %reshape.188 = bf16[2048,448]{0,1:T(8,128)(2,1)} reshape(bf16[4,2,256,448]{2,1,0,3:T(2,128)(2,1)} %copy.109) | data formatting | bytes 3670016 | tf_op jit(solution)/shard_map/reshape | solution.py:47
  248.7 2.3 convolution_add_fusion.3
  252.8 1.3 multiply_reduce_fusion
  260.2 1.3 copy.112
  261.8 2.0 fusion.2
  263.8 2.0 fusion.3
  266.2 2.4 copy.114
  268.6 1.7 copy.115
  270.3 31.5 %all_to_all.41 = bf16[4,8,2,128,128]{3,4,1,2,0:T(8,128)(2,1)S(1)} all-to-all(bf16[4,8,2,128,128]{3,4,1,2,0:T(8,128)(2,1)S(1)} %copy.115), channel_id=1, replica_groups=mesh['zh'=2,'y'=4,'c'=2,'x'=4,'zl'=8] {'x'}, dimensions={0} | all-to-all | bytes 4194304 | tf_op jit(solution)/shard_map/all_to_all | solution.py:83
  302.4 13.2 %all-to-all-start.7 = ((f32[16,1,448]{2,1,0:T(1,128)}), f32[16,1,448]{2,1,0:T(1,128)S(1)}, u32[]{:S(2)}, u32[]{:S(2)}) async-start(f32[16,1,448]{2,1,0:T(1,128)} %broadcast_in_dim.17), calls=%async_computation.7 | async-start | bytes 65536 | tf_op jit(solution)/shard_map/all_to_all | solution.py:12
  317.0 11.6 %all-to-all-done.7 = f32[16,1,448]{2,1,0:T(1,128)S(1)} async-done(((f32[16,1,448]{2,1,0:T(1,128)}), f32[16,1,448]{2,1,0:T(1,128)S(1)}, u32[]{:S(2)}, u32[]{:S(2)}) %all-to-all-start.7) | async-done | bytes 28704 | tf_op jit(solution)/shard_map/all_to_all | solution.py:12
  328.6 11.8 %all-to-all-start.6 = ((bf16[8,2,128,128]{2,3,1,0:T(8,128)(2,1)}), bf16[8,2,128,128]{2,3,1,0:T(8,128)(2,1)S(1)}, u32[]{:S(2)}, u32[]{:S(2)}) async-start(bf16[8,2,128,128]{2,3,1,0:T(8,128)(2,1)} %copy.117), calls=%async_computation.6 | async-start | bytes 1048576 | tf_op jit(solution)/shard_map/all_to_all | solution.py:85
  341.0 28.4 %all-to-all-done.6 = bf16[8,2,128,128]{2,3,1,0:T(8,128)(2,1)S(1)} async-done(((bf16[8,2,128,128]{2,3,1,0:T(8,128)(2,1)}), bf16[8,2,128,128]{2,3,1,0:T(8,128)(2,1)S(1)}, u32[]{:S(2)}, u32[]{:S(2)}) %all-to-all-start.6) | async-done | bytes 524320 | tf_op jit(solution)/shard_map/all_to_all | solution.py:85
  (66 shorter events, 18.5 us)
Async XLA Ops:
  0.6 29.2 %collective-permute-start.2 = (bf16[256,448]{0,1:T(8,128)(2,1)}, bf16[256,448]{0,1:T(8,128)(2,1)S(1)}, u32[]{:S(2)}, u32[]{:S(2)}) collective-permute-start(bf16[256,448]{0,1:T(8,128)(2,1)} %param.8), channel_id=1, source_target_pairs={{0,256},{256,0},{1,257},{257,1},{2,258},{258,2},{3,259},{259,3},{4... | collective-permute-start | bytes 688136 | tf_op jit(solution)/shard_map/ppermute | solution.py:16
  16.4 25.7 %collective-permute-start.4 = (bf16[256,448]{0,1:T(8,128)(2,1)}, bf16[256,448]{0,1:T(8,128)(2,1)S(1)}, u32[]{:S(2)}, u32[]{:S(2)}) collective-permute-start(bf16[256,448]{0,1:T(8,128)(2,1)} %bitcast.101), channel_id=1, source_target_pairs={{0,256},{256,0},{1,257},{257,1},{2,258},{258,2},{3,259},{259,3},{4... | collective-permute-start | bytes 688136 | tf_op jit(solution)/shard_map/ppermute | solution.py:16
  44.6 5.2 %copy-start.11 = (bf16[256,448]{0,1:T(8,128)(2,1)S(1)}, bf16[256,448]{0,1:T(8,128)(2,1)}, u32[]{:S(2)}) copy-start(bf16[256,448]{0,1:T(8,128)(2,1)} %param.7) | copy-start | bytes 688132
  44.6 26.3 %all-to-all-start.3 = ((bf16[4,2,256,448]{2,3,1,0:T(8,128)(2,1)}), bf16[4,2,256,448]{2,3,1,0:T(8,128)(2,1)}, u32[]{:S(2)}, u32[]{:S(2)}) async-start(bf16[4,2,256,448]{2,3,1,0:T(8,128)(2,1)} %broadcast_in_dim.15), calls=%async_computation.3 | async-start | bytes 3670016 | tf_op jit(solution)/shard_map/all_to_all | solution.py:12
  49.9 17.8 %collective-permute-start = (bf16[256,448]{0,1:T(8,128)(2,1)S(1)}, bf16[256,448]{0,1:T(8,128)(2,1)S(1)}, u32[]{:S(2)}, u32[]{:S(2)}) collective-permute-start(bf16[256,448]{0,1:T(8,128)(2,1)S(1)} %copy-done.11), channel_id=1, source_target_pairs={{0,256},{256,0},{1,257},{257,1},{2,258},{258,2},{3,259},{259,3},{4... | collective-permute-start | bytes 688136 | tf_op jit(solution)/shard_map/ppermute | solution.py:16
  72.3 6.6 %copy-start.12 = (bf16[128,1,128]{2,0,1:T(8,128)(2,1)S(1)}, bf16[128,1,128]{2,0,1:T(8,128)(2,1)}, u32[]{:S(2)}) copy-start(bf16[128,1,128]{2,0,1:T(8,128)(2,1)} %param.11) | copy-start | bytes 98308
  72.3 6.6 %copy-start.13 = (bf16[128,1,128]{2,0,1:T(8,128)(2,1)S(1)}, bf16[128,1,128]{2,0,1:T(8,128)(2,1)}, u32[]{:S(2)}) copy-start(bf16[128,1,128]{2,0,1:T(8,128)(2,1)} %param.6) | copy-start | bytes 98308
  72.3 26.7 %all-to-all-start.2 = ((bf16[4,2,256,448]{2,3,1,0:T(8,128)(2,1)}), bf16[4,2,256,448]{2,3,1,0:T(8,128)(2,1)}, u32[]{:S(2)}, u32[]{:S(2)}) async-start(bf16[4,2,256,448]{2,3,1,0:T(8,128)(2,1)} %broadcast_in_dim.14), calls=%async_computation.2 | async-start | bytes 3670016 | tf_op jit(solution)/shard_map/all_to_all | solution.py:12
  99.9 49.2 %all-to-all-start = ((bf16[8,2,128,128]{2,3,1,0:T(8,128)(2,1)}), bf16[8,2,128,128]{2,3,1,0:T(8,128)(2,1)S(1)}, u32[]{:S(2)}, u32[]{:S(2)}) async-start(bf16[8,2,128,128]{2,3,1,0:T(8,128)(2,1)} %broadcast_in_dim.12), calls=%async_computation | async-start | bytes 1048576 | tf_op jit(solution)/shard_map/all_to_all | solution.py:12
  150.5 20.0 %all-to-all-start.4 = ((bf16[4,2,256,448]{2,3,1,0:T(8,128)(2,1)}), bf16[4,2,256,448]{2,3,1,0:T(8,128)(2,1)}, u32[]{:S(2)}, u32[]{:S(2)}) async-start(bf16[4,2,256,448]{2,3,1,0:T(8,128)(2,1)} %broadcast_in_dim.16), calls=%async_computation.4 | async-start | bytes 3670016 | tf_op jit(solution)/shard_map/all_to_all | solution.py:12
  172.3 39.9 %all-to-all-start.1 = ((bf16[4,8,2,128,128]{3,4,1,2,0:T(8,128)(2,1)}), bf16[4,8,2,128,128]{3,4,1,2,0:T(8,128)(2,1)}, u32[]{:S(2)}, u32[]{:S(2)}) async-start(bf16[4,8,2,128,128]{3,4,1,2,0:T(8,128)(2,1)} %broadcast_in_dim.13), calls=%async_computation.1 | async-start | bytes 4194304 | tf_op jit(solution)/shard_map/all_to_all | solution.py:12
  176.8 42.2 %collective-permute-start.3 = (bf16[4,2,256,448]{2,3,1,0:T(8,128)(2,1)}, bf16[4,2,256,448]{2,3,1,0:T(8,128)(2,1)}, u32[]{:S(2)}, u32[]{:S(2)}) collective-permute-start(bf16[4,2,256,448]{2,3,1,0:T(8,128)(2,1)} %all-to-all-done.3), channel_id=1, source_target_pairs={{0,32},{32,0},{1,33},{33,1},{2,34},{34,2},{3,35},{35,3},{4,36},{36... | collective-permute-start | bytes 5505032 | tf_op jit(solution)/shard_map/ppermute | solution.py:16
  178.7 50.2 %collective-permute-start.1 = (bf16[4,2,256,448]{2,3,1,0:T(8,128)(2,1)}, bf16[4,2,256,448]{2,3,1,0:T(8,128)(2,1)}, u32[]{:S(2)}, u32[]{:S(2)}) collective-permute-start(bf16[4,2,256,448]{2,3,1,0:T(8,128)(2,1)} %all-to-all-done.2), channel_id=1, source_target_pairs={{0,32},{32,0},{1,33},{33,1},{2,34},{34,2},{3,35},{35,3},{4,36},{36... | collective-permute-start | bytes 5505032 | tf_op jit(solution)/shard_map/ppermute | solution.py:16
  181.1 57.7 %collective-permute-start.5 = (bf16[4,2,256,448]{2,3,1,0:T(8,128)(2,1)}, bf16[4,2,256,448]{2,3,1,0:T(8,128)(2,1)}, u32[]{:S(2)}, u32[]{:S(2)}) collective-permute-start(bf16[4,2,256,448]{2,3,1,0:T(8,128)(2,1)} %all-to-all-done.4), channel_id=1, source_target_pairs={{0,32},{32,0},{1,33},{33,1},{2,34},{34,2},{3,35},{35,3},{4,36},{36... | collective-permute-start | bytes 5505032 | tf_op jit(solution)/shard_map/ppermute | solution.py:16
  214.3 2.5 copy-start.6
  214.3 1.9 copy-start.3
  216.1 1.5 copy-start.5
  248.7 2.3 copy-start
  251.0 1.2 copy-start.7
  251.0 1.8 copy-start.8
  251.0 1.8 copy-start.9
  251.0 1.8 copy-start.14
  252.8 1.5 copy-start.4
  254.2 1.5 copy-start.2
  256.7 2.3 copy-start.1
  260.2 1.6 copy-start.10
  302.4 26.1 %all-to-all-start.7 = ((f32[16,1,448]{2,1,0:T(1,128)}), f32[16,1,448]{2,1,0:T(1,128)S(1)}, u32[]{:S(2)}, u32[]{:S(2)}) async-start(f32[16,1,448]{2,1,0:T(1,128)} %broadcast_in_dim.17), calls=%async_computation.7 | async-start | bytes 65536 | tf_op jit(solution)/shard_map/all_to_all | solution.py:12
  328.6 40.8 %all-to-all-start.6 = ((bf16[8,2,128,128]{2,3,1,0:T(8,128)(2,1)}), bf16[8,2,128,128]{2,3,1,0:T(8,128)(2,1)S(1)}, u32[]{:S(2)}, u32[]{:S(2)}) async-start(bf16[8,2,128,128]{2,3,1,0:T(8,128)(2,1)} %copy.117), calls=%async_computation.6 | async-start | bytes 1048576 | tf_op jit(solution)/shard_map/all_to_all | solution.py:85

commit v2 on v1

v2 whole, which is shorter than its diff:
```python
import jax
import jax.numpy as jnp
from jax import lax
from jax.experimental import pallas as pl
from jax.experimental.pallas import tpu as pltpu
from jax.sharding import Mesh, PartitionSpec as P

ROWS_AXES = ("zh", "y", "c")
COLS_AXES = ("x", "zl")
F32 = jnp.float32
BF16 = jnp.bfloat16


def spread(block, axis, size):
    copies = jnp.broadcast_to(block[None], (size,) + block.shape)
    return lax.all_to_all(copies, axis, 0, 0, tiled=True)


def shifted(block, axis, size):
    return [block] + [
        lax.ppermute(block, axis, [(i, (i + n) % size) for i in range(size)])
        for n in range(1, size)
    ]


def swap(block, axis):
    return lax.ppermute(block, axis, [(0, 1), (1, 0)])


def fetch(place, pairs, weights, sems):
    copies = []
    for pair in pairs:
        ny, matrices, _, depth = pair[0].shape
        for m in range(matrices):
            row = []
            for k, ref in enumerate(pair):
                core = jnp.bitwise_xor(place[1], k)
                for y in range(ny):
                    at = pl.multiple_of((y * 2 + core) * depth, depth)
                    copy = pltpu.make_async_copy(
                        ref.at[y, m],
                        weights.at[len(copies), :, pl.ds(at, depth)],
                        sems.at[len(copies), k * ny + y],
                    )
                    copy.start()
                    row.append(copy)
            copies.append(row)
    return copies


def near_kernel(
    place,
    acts_0, acts_1, acts_2, acts_3,
    own, core,
    part,
    tok_far,
    tok,
    weights,
    sems,
):
    acts = (acts_0, acts_1, acts_2, acts_3)
    nx = len(acts)
    nl, _, rows, width = acts_0.shape
    zh, me = place[0], place[2]
    copies = fetch(place, [(own, core)], weights, sems)

    for n in range(nx):
        x = lax.rem(me - n + nx, nx)
        base = lax.rem(x, nx // 2) * (nl * width)
        far = jnp.bitwise_xor(x // (nx // 2), zh)
        for zl in range(nl):
            at = pl.multiple_of(base + zl * width, width)
            for t in range(2):
                tok[far, t, :, pl.ds(at, width)] = acts[n][zl, t]
    tok_far[...] = tok[1]

    for m in range(3):
        for copy in copies[m]:
            copy.wait()
        part[m] = lax.dot_general(
            tok[0, m // 2], weights[m], (((1,), (1,)), ((), ())), preferred_element_type=F32
        )


def layer_kernel(
    place,
    part,
    tok_far,
    scale,
    near_own, near_core,
    first_own, first_core, last_own, last_core,
    outs,
    grad,
    near,
    far,
    sems,
):
    nx, nl, _, rows, width = outs.shape
    zh = place[0]
    far_copies = fetch(place, [(first_own, first_core), (last_own, last_core)], far, sems.at[1])
    near_copies = fetch(place, [(near_own, near_core)], near, sems.at[0])

    def times(t, m):
        for copy in far_copies[m]:
            copy.wait()
        return part[m] + lax.dot_general(
            tok_far[t], far[m], (((1,), (1,)), ((), ())), preferred_element_type=F32
        )

    gate_pre = times(0, 0)
    up_proj = times(0, 1)
    back = times(1, 2)
    sigmoid_gate = jax.nn.sigmoid(gate_pre)
    swish_gate = gate_pre * sigmoid_gate
    activated = swish_gate * up_proj
    hidden = (activated * scale[...]).astype(BF16)
    grad[...] = jnp.sum(back * activated, axis=0, keepdims=True)
    hidden_grad = back * scale[...]
    gate_grad = (
        hidden_grad * up_proj * sigmoid_gate * (1.0 + gate_pre * (1.0 - sigmoid_gate))
    ).astype(BF16)
    up_grad = (hidden_grad * swish_gate).astype(BF16)

    for m in range(3):
        for copy in near_copies[m]:
            copy.wait()
    for k, weights in enumerate((far, near)):
        half = jnp.bitwise_xor(zh, 1 - k)
        for n in range(nx * nl // 4):
            columns = slice(2 * n * width, 2 * (n + 1) * width)
            mixed = jnp.dot(hidden, weights[2, :, columns], preferred_element_type=F32)
            back_in = jnp.dot(
                gate_grad, weights[0, :, columns], preferred_element_type=F32
            ) + jnp.dot(up_grad, weights[1, :, columns], preferred_element_type=F32)
            for side in range(2):
                x, zl = divmod(2 * n + side, nl)
                x = half * (nx // 2) + x
                piece = slice(side * width, (side + 1) * width)
                outs[x, zl, 0] = mixed[:, piece].astype(BF16)
                outs[x, zl, 1] = back_in[:, piece].astype(BF16)


def whole():
    return pl.BlockSpec(memory_space=pltpu.VMEM)


def anywhere():
    return pl.BlockSpec(memory_space=pl.ANY)


def near_layer(place, acts, weights):
    nx = len(acts)
    nl, _, rows, width = acts[0].shape
    ny, _, hid, depth = weights[0].shape
    half = nx * nl * width // 2
    return pl.pallas_call(
        near_kernel,
        out_shape=(
            jax.ShapeDtypeStruct((3, rows, hid), F32),
            jax.ShapeDtypeStruct((2, rows, half), BF16),
        ),
        in_specs=[pl.BlockSpec(memory_space=pltpu.SMEM)] + [whole()] * nx + [anywhere()] * 2,
        out_specs=(whole(), whole()),
        scratch_shapes=[
            pltpu.VMEM((2, 2, rows, half), BF16),
            pltpu.VMEM((3, hid, half), BF16),
            pltpu.SemaphoreType.DMA((3, 2 * ny)),
        ],
        compiler_params=pltpu.CompilerParams(vmem_limit_bytes=48 * 2**20),
        cost_estimate=pl.CostEstimate(
            flops=6 * rows * half * hid, bytes_accessed=6 * half * hid, transcendentals=0
        ),
    )(place, *acts, *weights)


def layer(place, part, tok_far, scale, weights, nx, nl):
    _, rows, half = tok_far.shape
    ny, _, hid, depth = weights[0].shape
    width = 2 * half // (nx * nl)
    return pl.pallas_call(
        layer_kernel,
        out_shape=(
            jax.ShapeDtypeStruct((nx, nl, 2, rows, width), BF16),
            jax.ShapeDtypeStruct((1, hid), F32),
        ),
        in_specs=[pl.BlockSpec(memory_space=pltpu.SMEM)] + [whole()] * 3 + [anywhere()] * 6,
        out_specs=(whole(), whole()),
        scratch_shapes=[
            pltpu.VMEM((3, hid, half), BF16),
            pltpu.VMEM((3, hid, half), BF16),
            pltpu.SemaphoreType.DMA((2, 3, 2 * ny)),
        ],
        compiler_params=pltpu.CompilerParams(vmem_limit_bytes=48 * 2**20),
        cost_estimate=pl.CostEstimate(
            flops=18 * rows * half * hid,
            bytes_accessed=12 * half * hid,
            transcendentals=rows * hid,
        ),
    )(place, part, tok_far, scale, *weights)


def total(blocks):
    wide = [block.astype(F32) for block in blocks]
    while len(wide) > 1:
        wide = [a + b for a, b in zip(wide[::2], wide[1::2])]
    return wide[0]


def make_per_device(size):
    ny, nx, nl = (size[a] for a in ("y", "x", "zl"))

    def per_device(tokens, gate_weight, up_weight, down_weight, ia3_scale, cotangent):
        seq_len, seq_local, width = tokens.shape
        rows = seq_len * seq_local
        place = jnp.stack([lax.axis_index(a) for a in ("zh", "c", "x")])

        acts = jnp.stack([tokens.reshape(rows, width), cotangent.reshape(rows, width)])
        acts = spread(acts, "zl", nl)

        mine = [gate_weight.T, up_weight.T, down_weight]
        mine, acts = lax.optimization_barrier((mine, acts))
        first = [swap(w, "zh") for w in mine[:2]]
        near_own = spread(jnp.stack(mine), "y", ny)
        acts = shifted(acts, "x", nx)
        last = mine[2]
        acts, near_own, first, last = lax.optimization_barrier((acts, near_own, first, last))

        last = swap(last, "zh")
        first_own = spread(jnp.stack(first), "y", ny)
        near_core = swap(near_own, "c")
        part, tok_far = near_layer(place, acts, (near_own, near_core))
        first_own, last, part = lax.optimization_barrier((first_own, last, part))

        first_core = swap(first_own, "c")
        last_own = spread(last[None], "y", ny)
        last_core = swap(last_own, "c")
        weights = (near_own, near_core, first_own, first_core, last_own, last_core)
        outs, grad = layer(place, part, tok_far, ia3_scale.reshape(1, -1), weights, nx, nl)

        grad = grad + swap(grad, "c")
        grad = total(shifted(grad, "y", ny))

        outs = lax.all_to_all(outs, "x", 0, 0, tiled=True)
        outs = total([outs[i] for i in range(nx)]).astype(BF16)
        outs, grad = lax.optimization_barrier((outs, grad))
        scale_grad = (grad + swap(grad, "zh")).reshape(-1)
        outs = lax.all_to_all(outs, "zl", 0, 0, tiled=True)
        outs = total([outs[i] for i in range(nl)]).astype(BF16)
        return outs[0].reshape(tokens.shape), outs[1].reshape(tokens.shape), scale_grad

    return per_device


def solution(mesh):
    shape = {"zh": 2, "y": 4, "c": 2, "x": 4, "zl": 8}
    fine = Mesh(mesh.devices.reshape(tuple(shape.values())), tuple(shape))
    in_specs = (
        P(None, ROWS_AXES, COLS_AXES),
        P(ROWS_AXES, COLS_AXES),
        P(ROWS_AXES, COLS_AXES),
        P(COLS_AXES, ROWS_AXES),
        P(COLS_AXES),
        P(None, ROWS_AXES, COLS_AXES),
    )
    out_specs = (
        P(None, ROWS_AXES, COLS_AXES),
        P(None, ROWS_AXES, COLS_AXES),
        P(COLS_AXES),
    )
    return jax.shard_map(
        make_per_device(shape),
        mesh=fine,
        in_specs=in_specs,
        out_specs=out_specs,
        check_vma=False,
    )
```

time: 374 us -> 245 us (0.66)
  local copies, waits for them, and re-layouts: 82.8 us -> 12.6 us
  waiting for transfers between devices: 133 us -> 80.6 us
  starting transfers between devices: 107 us -> 74.5 us
  blocking collectives: 31.5 us -> 58.1 us
  matrix products: 13.5 us -> 0 us
  Pallas kernels: 0 us -> 12.3 us
    all_to_all x6 -> x2, waiting for transfers between devices: 75 us -> 2.12 us  [spread(): return lax.all_to_all(copies, axis, 0, 0, tiled=True)]
    all_to_all x6 -> x2, starting transfers between devices: 58.4 us -> 9.6 us  [spread(): return lax.all_to_all(copies, axis, 0, 0, tiled=True)]
    reshape x6 -> x0, local copies, waits for them, and re-layouts: 30.8 us -> none  [the longest x2 10.6 us: per_device(): down = [w.reshape(-1, hid) for w in gather(down_weight.T)]]
    all_to_all x1 -> x2, blocking collectives: 31.5 us -> 58.1 us  [spread(): return lax.all_to_all(copies, axis, 0, 0, tiled=True)]
    ppermute x6 -> x8, waiting for transfers between devices: 29.2 us -> 52.5 us  [swap(): return lax.ppermute(block, axis, [(0, 1), (1, 0)])]
    ppermute x0 -> x6, starting transfers between devices: none -> 20.6 us  [shifted(): lax.ppermute(block, axis, [(i, (i + n) % size) for i in range(size)])]
    all_to_all x5 -> x0, local copies, waits for them, and re-layouts: 15.8 us -> none  [spread(): return lax.all_to_all(copies, axis, 0, 0, tiled=True)]
    all_to_all x1, waiting for transfers between devices: 28.4 us -> 12.6 us  [per_device(): outs = lax.all_to_all(outs, 'zl', 0, 0, tiled=True)]
  transfers between devices with their start and end apart: 13 -> 18, of which waited for: 9 -> 10; matrix products, arithmetic and copies ran while one was open for 15% -> 1% of each run, Pallas kernels for 0% -> 2%
where the time goes in v2:
time: 245 us; the launch traced here: 243 us
  waiting for transfers between devices  80.6 us (33%)
  starting transfers between devices  74.5 us (30%)
  blocking collectives  58.1 us (24%)
  local copies, waits for them, and re-layouts  12.6 us (5%)
  Pallas kernels  12.3 us (5%)
  other arithmetic  3.92 us (2%)
    all_to_all x2, blocking collectives, spread(): return lax.all_to_all(copies, axis, 0, 0, tiled=True)  58.1 us
    ppermute x8, waiting for transfers between devices, swap(): return lax.ppermute(block, axis, [(0, 1), (1, 0)])  52.5 us
    ppermute x8, starting transfers between devices, swap(): return lax.ppermute(block, axis, [(0, 1), (1, 0)])  35.5 us
    ppermute x6, starting transfers between devices, shifted(): lax.ppermute(block, axis, [(i, (i + n) % size) for i in range(size)])  20.6 us
    all_to_all x1, waiting for transfers between devices, per_device(): outs = lax.all_to_all(outs, 'zl', 0, 0, tiled=True)  12.6 us
    all_to_all x1, waiting for transfers between devices, per_device(): outs = lax.all_to_all(outs, 'x', 0, 0, tiled=True)  11 us
    all_to_all x2, starting transfers between devices, spread(): return lax.all_to_all(copies, axis, 0, 0, tiled=True)  9.6 us
    pallas_call x1, Pallas kernels, layer(): pl.pallas_call(layer_kernel, out_shape=(jax.ShapeDtypeStruct((nx, nl, 2,...  7.82 us
  transfers between devices with their start and end apart: 18, of which 10 were waited for; matrix products, arithmetic and copies ran while one was open for 1% of the time, Pallas kernels for 2%

profile of v2, /device:TPU:24, one launch (start us, length us, event | category | flops | bytes accessed | tf_op | source)
XLA Modules:
  0.0 242.9 jit_solution(10864583816107755655)
XLA Ops:
  0.6 0.8 pad_maximum_fusion.2
  1.5 41.1 %all_to_all.30.acts_0 = bf16[8,2,128,128]{3,2,1,0:T(8,128)(2,1)S(1)} all-to-all(bf16[8,2,128,128]{3,2,1,0:T(8,128)(2,1)S(1)} %broadcast_in_dim.8), channel_id=1, replica_groups=mesh['zh'=2,'y'=4,'c'=2,'x'=4,'zl'=8] {'zl'}, dimensions={0} | all-to-all | bytes 1048576 | tf_op jit(solution)/shard_map/all_to_all | solution.py:16
  42.6 1.2 pad_maximum_fusion
  43.8 1.8 broadcast_in_dim.9
  45.6 4.9 %all-to-all-start.1 = ((bf16[4,3,448,256]{3,2,1,0:T(8,128)(2,1)}), bf16[4,3,448,256]{3,2,1,0:T(8,128)(2,1)}, u32[]{:S(2)}, u32[]{:S(2)}) async-start(bf16[4,3,448,256]{3,2,1,0:T(8,128)(2,1)} %broadcast_in_dim.9), calls=%async_computation.1 | async-start | bytes 5505024 | tf_op jit(solution)/shard_map/all_to_all | solution.py:16
  50.5 4.7 %collective-permute-start.2 = (bf16[8,2,128,128]{3,2,1,0:T(8,128)(2,1)S(1)}, bf16[8,2,128,128]{3,2,1,0:T(8,128)(2,1)S(1)}, u32[]{:S(2)}, u32[]{:S(2)}) collective-permute-start(bf16[8,2,128,128]{3,2,1,0:T(8,128)(2,1)S(1)} %all_to_all.30.acts_0), channel_id=1, source_target_pairs={{0,24},{8,0},{16,8},{24,16},{1,25},{9,1},{17,9},{25,17},{2,26},{10... | collective-permute-start | bytes 1572872 | tf_op jit(solution)/shard_map/ppermute | solution.py:21
  55.2 2.7 %collective-permute-start.1 = (bf16[8,2,128,128]{3,2,1,0:T(8,128)(2,1)S(1)}, bf16[8,2,128,128]{3,2,1,0:T(8,128)(2,1)S(1)}, u32[]{:S(2)}, u32[]{:S(2)}) collective-permute-start(bf16[8,2,128,128]{3,2,1,0:T(8,128)(2,1)S(1)} %all_to_all.30.acts_0), channel_id=1, source_target_pairs={{0,16},{8,24},{16,0},{24,8},{1,17},{9,25},{17,1},{25,9},{2,18},{10... | collective-permute-start | bytes 1572872 | tf_op jit(solution)/shard_map/ppermute | solution.py:21
  57.9 2.8 %collective-permute-start = (bf16[8,2,128,128]{3,2,1,0:T(8,128)(2,1)S(1)}, bf16[8,2,128,128]{3,2,1,0:T(8,128)(2,1)S(1)}, u32[]{:S(2)}, u32[]{:S(2)}) collective-permute-start(bf16[8,2,128,128]{3,2,1,0:T(8,128)(2,1)S(1)} %all_to_all.30.acts_0), channel_id=1, source_target_pairs={{0,8},{8,16},{16,24},{24,0},{1,9},{9,17},{17,25},{25,1},{2,10},{10... | collective-permute-start | bytes 1572872 | tf_op jit(solution)/shard_map/ppermute | solution.py:21
  60.7 8.2 %collective-permute-start.3 = (bf16[448,256]{1,0:T(8,128)(2,1)S(1)}, bf16[448,256]{1,0:T(8,128)(2,1)S(1)}, u32[]{:S(2)}, u32[]{:S(2)}) collective-permute-start(bf16[448,256]{1,0:T(8,128)(2,1)S(1)} %bitcast.24), channel_id=1, source_target_pairs={{0,256},{256,0},{1,257},{257,1},{2,258},{258,2},{3,259},{259,3},{4... | collective-permute-start | bytes 688136 | tf_op jit(solution)/shard_map/ppermute | solution.py:27
  68.9 6.3 %collective-permute-start.4 = (bf16[448,256]{1,0:T(8,128)(2,1)S(1)}, bf16[448,256]{1,0:T(8,128)(2,1)S(1)}, u32[]{:S(2)}, u32[]{:S(2)}) collective-permute-start(bf16[448,256]{1,0:T(8,128)(2,1)S(1)} %bitcast.26), channel_id=1, source_target_pairs={{0,256},{256,0},{1,257},{257,1},{2,258},{258,2},{3,259},{259,3},{4... | collective-permute-start | bytes 688136 | tf_op jit(solution)/shard_map/ppermute | solution.py:27
  75.3 33.1 %collective-permute-done.3 = bf16[448,256]{1,0:T(8,128)(2,1)S(1)} collective-permute-done((bf16[448,256]{1,0:T(8,128)(2,1)S(1)}, bf16[448,256]{1,0:T(8,128)(2,1)S(1)}, u32[]{:S(2)}, u32[]{:S(2)}) %collective-permute-start.3) | collective-permute-done | bytes 229408 | tf_op jit(solution)/shard_map/ppermute | solution.py:27
  108.4 2.5 %collective-permute-done.4 = bf16[448,256]{1,0:T(8,128)(2,1)S(1)} collective-permute-done((bf16[448,256]{1,0:T(8,128)(2,1)S(1)}, bf16[448,256]{1,0:T(8,128)(2,1)S(1)}, u32[]{:S(2)}, u32[]{:S(2)}) %collective-permute-start.4) | collective-permute-done | bytes 229408 | tf_op jit(solution)/shard_map/ppermute | solution.py:27
  110.9 0.8 copy-done.2
  111.7 0.8 copy-done.4
  112.5 0.8 copy-done.6
  113.3 1.9 collective-permute-start.6
  115.3 1.4 broadcast_in_dim.10
  116.7 4.7 %all-to-all-start.2 = ((bf16[4,2,448,256]{3,2,1,0:T(8,128)(2,1)}), bf16[4,2,448,256]{3,2,1,0:T(8,128)(2,1)S(1)}, u32[]{:S(2)}, u32[]{:S(2)}) async-start(bf16[4,2,448,256]{3,2,1,0:T(8,128)(2,1)} %broadcast_in_dim.10), calls=%async_computation.2 | async-start | bytes 3670016 | tf_op jit(solution)/shard_map/all_to_all | solution.py:16
  121.4 6.3 %collective-permute-start.5 = (bf16[448,256]{1,0:T(8,128)(2,1)}, bf16[448,256]{1,0:T(8,128)(2,1)}, u32[]{:S(2)}, u32[]{:S(2)}) collective-permute-start(bf16[448,256]{1,0:T(8,128)(2,1)} %param.9), channel_id=1, source_target_pairs={{0,256},{256,0},{1,257},{257,1},{2,258},{258,2},{3,259},{259,3},{4... | collective-permute-start | bytes 688136 | tf_op jit(solution)/shard_map/ppermute | solution.py:27
  127.8 1.0 copy-done.3
  128.8 1.0 copy-done.5
  129.9 1.0 copy-done.7
  130.9 4.5 %shard_map.85 = (f32[3,128,448]{2,1,0:T(8,128)S(1)}, bf16[2,128,2048]{2,1,0:T(8,128)(2,1)S(1)}) custom-call(s32[3]{0:T(128)S(1)} %pad_add_fusion.place, bf16[8,2,128,128]{3,2,1,0:T(8,128)(2,1)S(1)} %all_to_all.30.acts_0, bf16[8,2,128,128]{3,2,1,0:T(8,128)(2,1)S(1)} %copy-done.7, bf16[8,2,128,128]{3,2,1,0:T(8,128)(2,1)S(1)} %copy-done.5, ...), custom_call_target="tpu_custom_call" | custom-call | flops 704643072 | bytes 5505024 | tf_op jit(solution)/shard_map/pallas_call | solution.py:156
  135.4 0.9 copy-done
  136.3 5.1 %collective-permute-done.5 = bf16[448,256]{1,0:T(8,128)(2,1)} collective-permute-done((bf16[448,256]{1,0:T(8,128)(2,1)}, bf16[448,256]{1,0:T(8,128)(2,1)}, u32[]{:S(2)}, u32[]{:S(2)}) %collective-permute-start.5) | collective-permute-done | bytes 229408 | tf_op jit(solution)/shard_map/ppermute | solution.py:27
  141.4 2.1 all-to-all-done.2.first_own
  143.5 2.0 collective-permute-start.7
  145.6 1.0 broadcast_in_dim.11
  146.6 17.0 %all_to_all.31.last_own = bf16[4,1,448,256]{3,2,1,0:T(8,128)(2,1)S(1)} all-to-all(bf16[4,1,448,256]{3,2,1,0:T(8,128)(2,1)S(1)} %broadcast_in_dim.11), channel_id=1, replica_groups=mesh['zh'=2,'y'=4,'c'=2,'x'=4,'zl'=8] {'y'}, dimensions={0} | all-to-all | bytes 1835008 | tf_op jit(solution)/shard_map/all_to_all | solution.py:16
  163.6 1.9 collective-permute-start.8
  165.6 2.4 %collective-permute-done.8.last_core = bf16[4,1,448,256]{3,2,1,0:T(8,128)(2,1)S(1)} collective-permute-done((bf16[4,1,448,256]{3,2,1,0:T(8,128)(2,1)S(1)}, bf16[4,1,448,256]{3,2,1,0:T(8,128)(2,1)S(1)}, u32[]{:S(2)}, u32[]{:S(2)}) %collective-permute-start.8) | collective-permute-done | bytes 917536 | tf_op jit(solution)/shard_map/ppermute | solution.py:27
  168.0 1.2 copy-done.9
  169.2 7.8 %shard_map.86 = (bf16[4,8,2,128,128]{4,3,2,1,0:T(8,128)(2,1)}, f32[1,448]{1,0:T(1,128)S(1)}) custom-call(s32[3]{0:T(128)S(1)} %pad_add_fusion.place, f32[3,128,448]{2,1,0:T(8,128)S(1)} %copy-done.1, bf16[2,128,2048]{2,1,0:T(8,128)(2,1)S(1)} %get-tuple-element.38.tok_far, f32[1,448]{1,0:T(1,128)S(1)} %bitcast.20, ...), custom_call_target="tpu_custom_call" | custom-call | flops 2113929216 | bytes 11010048 | tf_op jit(solution)/shard_map/pallas_call | solution.py:180
  177.1 3.6 %all-to-all-start.4 = ((bf16[4,8,2,128,128]{4,3,2,1,0:T(8,128)(2,1)}), bf16[4,8,2,128,128]{4,3,2,1,0:T(8,128)(2,1)S(1)}, u32[]{:S(2)}, u32[]{:S(2)}) async-start(bf16[4,8,2,128,128]{4,3,2,1,0:T(8,128)(2,1)} %get-tuple-element.41), calls=%async_computation.4 | async-start | bytes 4194304 | tf_op jit(solution)/shard_map/all_to_all | solution.py:243
  180.7 2.0 collective-permute-start.9
  182.8 1.0 collective-permute-done.9
  183.8 2.1 collective-permute-start.12
  185.9 5.2 %collective-permute-start.11 = (f32[1,448]{1,0:T(1,128)S(1)}, f32[1,448]{1,0:T(1,128)S(1)}, u32[]{:S(2)}, u32[]{:S(2)}) collective-permute-start(f32[1,448]{1,0:T(1,128)S(1)} %add.58), channel_id=1, source_target_pairs={{0,128},{64,192},{128,0},{192,64},{1,129},{65,193},{129,1},{193,65... | collective-permute-start | bytes 5384 | tf_op jit(solution)/shard_map/ppermute | solution.py:21
  191.1 3.1 %collective-permute-start.10 = (f32[1,448]{1,0:T(1,128)S(1)}, f32[1,448]{1,0:T(1,128)S(1)}, u32[]{:S(2)}, u32[]{:S(2)}) collective-permute-start(f32[1,448]{1,0:T(1,128)S(1)} %add.58), channel_id=1, source_target_pairs={{0,64},{64,128},{128,192},{192,0},{1,65},{65,129},{129,193},{193,1... | collective-permute-start | bytes 5384 | tf_op jit(solution)/shard_map/ppermute | solution.py:21
  194.2 2.4 collective-permute-done.10
  196.6 11.0 %all-to-all-done.4 = bf16[4,8,2,128,128]{4,3,2,1,0:T(8,128)(2,1)S(1)} async-done(((bf16[4,8,2,128,128]{4,3,2,1,0:T(8,128)(2,1)}), bf16[4,8,2,128,128]{4,3,2,1,0:T(8,128)(2,1)S(1)}, u32[]{:S(2)}, u32[]{:S(2)}) %all-to-all-start.4) | async-done | bytes 2097184 | tf_op jit(solution)/shard_map/all_to_all | solution.py:243
  207.6 1.1 fusion
  208.7 5.1 %all-to-all-start.5 = ((bf16[8,2,128,128]{3,2,1,0:T(8,128)(2,1)}), bf16[8,2,128,128]{3,2,1,0:T(8,128)(2,1)S(1)}, u32[]{:S(2)}, u32[]{:S(2)}) async-start(bf16[8,2,128,128]{3,2,1,0:T(8,128)(2,1)} %fusion), calls=%async_computation.5 | async-start | bytes 1048576 | tf_op jit(solution)/shard_map/all_to_all | solution.py:247
  213.8 6.8 %collective-permute-start.13 = (f32[1,448]{1,0:T(1,128)S(1)}, f32[1,448]{1,0:T(1,128)S(1)}, u32[]{:S(2)}, u32[]{:S(2)}) collective-permute-start(f32[1,448]{1,0:T(1,128)S(1)} %add_add_fusion), channel_id=1, source_target_pairs={{0,256},{256,0},{1,257},{257,1},{2,258},{258,2},{3,259},{259,3},{4... | collective-permute-start | bytes 5384 | tf_op jit(solution)/shard_map/ppermute | solution.py:27
  220.6 8.3 %collective-permute-done.13 = f32[1,448]{1,0:T(1,128)S(1)} collective-permute-done((f32[1,448]{1,0:T(1,128)S(1)}, f32[1,448]{1,0:T(1,128)S(1)}, u32[]{:S(2)}, u32[]{:S(2)}) %collective-permute-start.13) | collective-permute-done | bytes 1824 | tf_op jit(solution)/shard_map/ppermute | solution.py:27
  228.9 0.6 add.69
  229.5 12.6 %all-to-all-done.5 = bf16[8,2,128,128]{3,2,1,0:T(8,128)(2,1)S(1)} async-done(((bf16[8,2,128,128]{3,2,1,0:T(8,128)(2,1)}), bf16[8,2,128,128]{3,2,1,0:T(8,128)(2,1)S(1)}, u32[]{:S(2)}, u32[]{:S(2)}) %all-to-all-start.5) | async-done | bytes 524320 | tf_op jit(solution)/shard_map/all_to_all | solution.py:247
  242.2 0.6 slice_bitcast_fusion
  (30 shorter events, 0.3 us)
Async XLA Ops:
  45.6 15.1 %copy-start.10 = (bf16[256,448]{0,1:T(8,128)(2,1)S(1)}, bf16[256,448]{0,1:T(8,128)(2,1)}, u32[]{:S(2)}) copy-start(bf16[256,448]{0,1:T(8,128)(2,1)} %param.7) | copy-start | bytes 688132
  45.6 23.3 %copy-start.11 = (bf16[256,448]{0,1:T(8,128)(2,1)S(1)}, bf16[256,448]{0,1:T(8,128)(2,1)}, u32[]{:S(2)}) copy-start(bf16[256,448]{0,1:T(8,128)(2,1)} %param.8) | copy-start | bytes 688132
  45.6 67.7 %all-to-all-start.1 = ((bf16[4,3,448,256]{3,2,1,0:T(8,128)(2,1)}), bf16[4,3,448,256]{3,2,1,0:T(8,128)(2,1)}, u32[]{:S(2)}, u32[]{:S(2)}) async-start(bf16[4,3,448,256]{3,2,1,0:T(8,128)(2,1)} %broadcast_in_dim.9), calls=%async_computation.1 | async-start | bytes 5505024 | tf_op jit(solution)/shard_map/all_to_all | solution.py:16
  50.5 60.4 %collective-permute-start.2 = (bf16[8,2,128,128]{3,2,1,0:T(8,128)(2,1)S(1)}, bf16[8,2,128,128]{3,2,1,0:T(8,128)(2,1)S(1)}, u32[]{:S(2)}, u32[]{:S(2)}) collective-permute-start(bf16[8,2,128,128]{3,2,1,0:T(8,128)(2,1)S(1)} %all_to_all.30.acts_0), channel_id=1, source_target_pairs={{0,24},{8,0},{16,8},{24,16},{1,25},{9,1},{17,9},{25,17},{2,26},{10... | collective-permute-start | bytes 1572872 | tf_op jit(solution)/shard_map/ppermute | solution.py:21
  55.2 56.5 %collective-permute-start.1 = (bf16[8,2,128,128]{3,2,1,0:T(8,128)(2,1)S(1)}, bf16[8,2,128,128]{3,2,1,0:T(8,128)(2,1)S(1)}, u32[]{:S(2)}, u32[]{:S(2)}) collective-permute-start(bf16[8,2,128,128]{3,2,1,0:T(8,128)(2,1)S(1)} %all_to_all.30.acts_0), channel_id=1, source_target_pairs={{0,16},{8,24},{16,0},{24,8},{1,17},{9,25},{17,1},{25,9},{2,18},{10... | collective-permute-start | bytes 1572872 | tf_op jit(solution)/shard_map/ppermute | solution.py:21
  57.9 54.6 %collective-permute-start = (bf16[8,2,128,128]{3,2,1,0:T(8,128)(2,1)S(1)}, bf16[8,2,128,128]{3,2,1,0:T(8,128)(2,1)S(1)}, u32[]{:S(2)}, u32[]{:S(2)}) collective-permute-start(bf16[8,2,128,128]{3,2,1,0:T(8,128)(2,1)S(1)} %all_to_all.30.acts_0), channel_id=1, source_target_pairs={{0,8},{8,16},{16,24},{24,0},{1,9},{9,17},{17,25},{25,1},{2,10},{10... | collective-permute-start | bytes 1572872 | tf_op jit(solution)/shard_map/ppermute | solution.py:21
  60.7 47.7 %collective-permute-start.3 = (bf16[448,256]{1,0:T(8,128)(2,1)S(1)}, bf16[448,256]{1,0:T(8,128)(2,1)S(1)}, u32[]{:S(2)}, u32[]{:S(2)}) collective-permute-start(bf16[448,256]{1,0:T(8,128)(2,1)S(1)} %bitcast.24), channel_id=1, source_target_pairs={{0,256},{256,0},{1,257},{257,1},{2,258},{258,2},{3,259},{259,3},{4... | collective-permute-start | bytes 688136 | tf_op jit(solution)/shard_map/ppermute | solution.py:27
  68.9 42.0 %collective-permute-start.4 = (bf16[448,256]{1,0:T(8,128)(2,1)S(1)}, bf16[448,256]{1,0:T(8,128)(2,1)S(1)}, u32[]{:S(2)}, u32[]{:S(2)}) collective-permute-start(bf16[448,256]{1,0:T(8,128)(2,1)S(1)} %bitcast.26), channel_id=1, source_target_pairs={{0,256},{256,0},{1,257},{257,1},{2,258},{258,2},{3,259},{259,3},{4... | collective-permute-start | bytes 688136 | tf_op jit(solution)/shard_map/ppermute | solution.py:27
  110.9 0.8 copy-start.2
  111.7 0.8 copy-start.4
  112.5 0.8 copy-start.6
  113.3 14.5 %collective-permute-start.6 = (bf16[4,3,448,256]{3,2,1,0:T(8,128)(2,1)}, bf16[4,3,448,256]{3,2,1,0:T(8,128)(2,1)}, u32[]{:S(2)}, u32[]{:S(2)}) collective-permute-start(bf16[4,3,448,256]{3,2,1,0:T(8,128)(2,1)} %all-to-all-done.1.own.near_own), channel_id=1, source_target_pairs={{0,32},{32,0},{1,33},{33,1},{2,34},{34,2},{3,35},{35,3},{4,36},{36... | collective-permute-start | bytes 8257544 | tf_op jit(solution)/shard_map/ppermute | solution.py:27
  116.7 26.8 %all-to-all-start.2 = ((bf16[4,2,448,256]{3,2,1,0:T(8,128)(2,1)}), bf16[4,2,448,256]{3,2,1,0:T(8,128)(2,1)S(1)}, u32[]{:S(2)}, u32[]{:S(2)}) async-start(bf16[4,2,448,256]{3,2,1,0:T(8,128)(2,1)} %broadcast_in_dim.10), calls=%async_computation.2 | async-start | bytes 3670016 | tf_op jit(solution)/shard_map/all_to_all | solution.py:16
  121.4 20.0 %collective-permute-start.5 = (bf16[448,256]{1,0:T(8,128)(2,1)}, bf16[448,256]{1,0:T(8,128)(2,1)}, u32[]{:S(2)}, u32[]{:S(2)}) collective-permute-start(bf16[448,256]{1,0:T(8,128)(2,1)} %param.9), channel_id=1, source_target_pairs={{0,256},{256,0},{1,257},{257,1},{2,258},{258,2},{3,259},{259,3},{4... | collective-permute-start | bytes 688136 | tf_op jit(solution)/shard_map/ppermute | solution.py:27
  127.8 1.0 copy-start.3
  128.8 1.0 copy-start.5
  129.9 1.0 copy-start.7
  135.4 0.9 copy-start
  136.3 33.0 %copy-start.8 = (f32[448]{0:T(512)S(1)}, f32[448]{0:T(512)}, u32[]{:S(2)}) copy-start(f32[448]{0:T(512)} %param.10) | copy-start | bytes 5380
  143.5 25.7 %copy-start.1 = (f32[3,128,448]{2,1,0:T(8,128)S(1)}, f32[3,128,448]{2,1,0:T(8,128)}, u32[]{:S(2)}) copy-start(f32[3,128,448]{2,1,0:T(8,128)} %copy-done) | copy-start | bytes 2064388
  143.5 24.5 %collective-permute-start.7 = (bf16[4,2,448,256]{3,2,1,0:T(8,128)(2,1)S(1)}, bf16[4,2,448,256]{3,2,1,0:T(8,128)(2,1)S(1)}, u32[]{:S(2)}, u32[]{:S(2)}) collective-permute-start(bf16[4,2,448,256]{3,2,1,0:T(8,128)(2,1)S(1)} %all-to-all-done.2.first_own), channel_id=1, source_target_pairs={{0,32},{32,0},{1,33},{33,1},{2,34},{34,2},{3,35},{35,3},{4,36},{36... | collective-permute-start | bytes 5505032 | tf_op jit(solution)/shard_map/ppermute | solution.py:27
  163.6 4.4 %collective-permute-start.8 = (bf16[4,1,448,256]{3,2,1,0:T(8,128)(2,1)S(1)}, bf16[4,1,448,256]{3,2,1,0:T(8,128)(2,1)S(1)}, u32[]{:S(2)}, u32[]{:S(2)}) collective-permute-start(bf16[4,1,448,256]{3,2,1,0:T(8,128)(2,1)S(1)} %all_to_all.31.last_own), channel_id=1, source_target_pairs={{0,32},{32,0},{1,33},{33,1},{2,34},{34,2},{3,35},{35,3},{4,36},{36... | collective-permute-start | bytes 2752520 | tf_op jit(solution)/shard_map/ppermute | solution.py:27
  168.0 1.2 copy-start.9
  177.1 30.5 %all-to-all-start.4 = ((bf16[4,8,2,128,128]{4,3,2,1,0:T(8,128)(2,1)}), bf16[4,8,2,128,128]{4,3,2,1,0:T(8,128)(2,1)S(1)}, u32[]{:S(2)}, u32[]{:S(2)}) async-start(bf16[4,8,2,128,128]{4,3,2,1,0:T(8,128)(2,1)} %get-tuple-element.41), calls=%async_computation.4 | async-start | bytes 4194304 | tf_op jit(solution)/shard_map/all_to_all | solution.py:243
  180.7 3.0 %collective-permute-start.9 = (f32[1,448]{1,0:T(1,128)S(1)}, f32[1,448]{1,0:T(1,128)S(1)}, u32[]{:S(2)}, u32[]{:S(2)}) collective-permute-start(f32[1,448]{1,0:T(1,128)S(1)} %get-tuple-element.42), channel_id=1, source_target_pairs={{0,32},{32,0},{1,33},{33,1},{2,34},{34,2},{3,35},{35,3},{4,36},{36... | collective-permute-start | bytes 5384 | tf_op jit(solution)/shard_map/ppermute | solution.py:27
  183.8 10.4 %collective-permute-start.12 = (f32[1,448]{1,0:T(1,128)S(1)}, f32[1,448]{1,0:T(1,128)S(1)}, u32[]{:S(2)}, u32[]{:S(2)}) collective-permute-start(f32[1,448]{1,0:T(1,128)S(1)} %add.58), channel_id=1, source_target_pairs={{0,192},{64,0},{128,64},{192,128},{1,193},{65,1},{129,65},{193,129... | collective-permute-start | bytes 5384 | tf_op jit(solution)/shard_map/ppermute | solution.py:21
  185.9 8.3 %collective-permute-start.11 = (f32[1,448]{1,0:T(1,128)S(1)}, f32[1,448]{1,0:T(1,128)S(1)}, u32[]{:S(2)}, u32[]{:S(2)}) collective-permute-start(f32[1,448]{1,0:T(1,128)S(1)} %add.58), channel_id=1, source_target_pairs={{0,128},{64,192},{128,0},{192,64},{1,129},{65,193},{129,1},{193,65... | collective-permute-start | bytes 5384 | tf_op jit(solution)/shard_map/ppermute | solution.py:21
  191.1 5.5 %collective-permute-start.10 = (f32[1,448]{1,0:T(1,128)S(1)}, f32[1,448]{1,0:T(1,128)S(1)}, u32[]{:S(2)}, u32[]{:S(2)}) collective-permute-start(f32[1,448]{1,0:T(1,128)S(1)} %add.58), channel_id=1, source_target_pairs={{0,64},{64,128},{128,192},{192,0},{1,65},{65,129},{129,193},{193,1... | collective-permute-start | bytes 5384 | tf_op jit(solution)/shard_map/ppermute | solution.py:21
  208.7 33.5 %all-to-all-start.5 = ((bf16[8,2,128,128]{3,2,1,0:T(8,128)(2,1)}), bf16[8,2,128,128]{3,2,1,0:T(8,128)(2,1)S(1)}, u32[]{:S(2)}, u32[]{:S(2)}) async-start(bf16[8,2,128,128]{3,2,1,0:T(8,128)(2,1)} %fusion), calls=%async_computation.5 | async-start | bytes 1048576 | tf_op jit(solution)/shard_map/all_to_all | solution.py:247
  213.8 15.1 %collective-permute-start.13 = (f32[1,448]{1,0:T(1,128)S(1)}, f32[1,448]{1,0:T(1,128)S(1)}, u32[]{:S(2)}, u32[]{:S(2)}) collective-permute-start(f32[1,448]{1,0:T(1,128)S(1)} %add_add_fusion), channel_id=1, source_target_pairs={{0,256},{256,0},{1,257},{257,1},{2,258},{258,2},{3,259},{259,3},{4... | collective-permute-start | bytes 5384 | tf_op jit(solution)/shard_map/ppermute | solution.py:27

commit v3 on v2

--- a/solution.py
+++ b/solution.py
@@ -6,14 +6,17 @@
 from jax.sharding import Mesh, PartitionSpec as P
 
 ROWS_AXES = ("zh", "y", "c")
-COLS_AXES = ("x", "zl")
+COLS_AXES = ("x", "zb", "za")
 F32 = jnp.float32
 BF16 = jnp.bfloat16
 
 
+def copies(block, size):
+    return jnp.broadcast_to(block[None], (size,) + block.shape)
+
+
 def spread(block, axis, size):
-    copies = jnp.broadcast_to(block[None], (size,) + block.shape)
-    return lax.all_to_all(copies, axis, 0, 0, tiled=True)
+    return lax.all_to_all(copies(block, size), axis, 0, 0, tiled=True)
 
 
 def shifted(block, axis, size):
@@ -28,23 +31,27 @@
 
 
 def fetch(place, pairs, weights, sems):
-    copies = []
+    matrices, hid, _ = weights.shape
+    copies = [[] for _ in range(matrices)]
+    row, part = 0, 0
     for pair in pairs:
-        ny, matrices, _, depth = pair[0].shape
-        for m in range(matrices):
-            row = []
+        ny, height, depth = pair[0].shape
+        start = 0
+        while start < height:
+            m, first = divmod(row, hid)
+            count = min(hid - first, height - start)
             for k, ref in enumerate(pair):
                 core = jnp.bitwise_xor(place[1], k)
                 for y in range(ny):
                     at = pl.multiple_of((y * 2 + core) * depth, depth)
                     copy = pltpu.make_async_copy(
-                        ref.at[y, m],
-                        weights.at[len(copies), :, pl.ds(at, depth)],
-                        sems.at[len(copies), k * ny + y],
+                        ref.at[y, pl.ds(start, count)],
+                        weights.at[m, pl.ds(first, count), pl.ds(at, depth)],
+                        sems.at[part, k * ny + y],
                     )
                     copy.start()
-                    row.append(copy)
-            copies.append(row)
+                    copies[m].append(copy)
+            start, row, part = start + count, row + count, part + 1
     return copies
 
 
@@ -60,18 +67,20 @@
 ):
     acts = (acts_0, acts_1, acts_2, acts_3)
     nx = len(acts)
-    nl, _, rows, width = acts_0.shape
+    na, nb, _, rows, width = acts_0.shape
     zh, me = place[0], place[2]
     copies = fetch(place, [(own, core)], weights, sems)
 
     for n in range(nx):
         x = lax.rem(me - n + nx, nx)
-        base = lax.rem(x, nx // 2) * (nl * width)
+        base = lax.rem(x, nx // 2) * (nb * na)
         far = jnp.bitwise_xor(x // (nx // 2), zh)
-        for zl in range(nl):
-            at = pl.multiple_of(base + zl * width, width)
-            for t in range(2):
-                tok[far, t, :, pl.ds(at, width)] = acts[n][zl, t]
+        for a in range(na):
+            for b in range(nb):
+                zl = jnp.bitwise_xor(place[3], b) * na + a
+                at = pl.multiple_of((base + zl) * width, width)
+                for t in range(2):
+                    tok[far, t, :, pl.ds(at, width)] = acts[n][a, b, t]
     tok_far[...] = tok[1]
 
     for m in range(3):
@@ -150,16 +159,17 @@
 
 def near_layer(place, acts, weights):
     nx = len(acts)
-    nl, _, rows, width = acts[0].shape
-    ny, _, hid, depth = weights[0].shape
-    half = nx * nl * width // 2
+    na, nb, _, rows, width = acts[0].shape
+    ny, height, _ = weights[0].shape
+    hid = height // 3
+    half = nx * na * nb * width // 2
     return pl.pallas_call(
         near_kernel,
         out_shape=(
             jax.ShapeDtypeStruct((3, rows, hid), F32),
             jax.ShapeDtypeStruct((2, rows, half), BF16),
         ),
-        in_specs=[pl.BlockSpec(memory_space=pltpu.SMEM)] + [whole()] * nx + [anywhere()] * 2,
+        in_specs=[pl.BlockSpec(memory_space=pltpu.SMEM)] + [whole()] * len(acts) + [anywhere()] * 2,
         out_specs=(whole(), whole()),
         scratch_shapes=[
             pltpu.VMEM((2, 2, rows, half), BF16),
@@ -175,7 +185,8 @@
 
 def layer(place, part, tok_far, scale, weights, nx, nl):
     _, rows, half = tok_far.shape
-    ny, _, hid, depth = weights[0].shape
+    ny, height, _ = weights[0].shape
+    hid = height // 3
     width = 2 * half // (nx * nl)
     return pl.pallas_call(
         layer_kernel,
@@ -188,7 +199,7 @@
         scratch_shapes=[
             pltpu.VMEM((3, hid, half), BF16),
             pltpu.VMEM((3, hid, half), BF16),
-            pltpu.SemaphoreType.DMA((2, 3, 2 * ny)),
+            pltpu.SemaphoreType.DMA((2, 4, 2 * ny)),
         ],
         compiler_params=pltpu.CompilerParams(vmem_limit_bytes=48 * 2**20),
         cost_estimate=pl.CostEstimate(
@@ -207,52 +218,58 @@
 
 
 def make_per_device(size):
-    ny, nx, nl = (size[a] for a in ("y", "x", "zl"))
+    ny, nx, nb, na = (size[a] for a in ("y", "x", "zb", "za"))
 
     def per_device(tokens, gate_weight, up_weight, down_weight, ia3_scale, cotangent):
         seq_len, seq_local, width = tokens.shape
         rows = seq_len * seq_local
-        place = jnp.stack([lax.axis_index(a) for a in ("zh", "c", "x")])
+        place = jnp.stack([lax.axis_index(a) for a in ("zh", "c", "x", "zb")])
 
         acts = jnp.stack([tokens.reshape(rows, width), cotangent.reshape(rows, width)])
-        acts = spread(acts, "zl", nl)
-
-        mine = [gate_weight.T, up_weight.T, down_weight]
-        mine, acts = lax.optimization_barrier((mine, acts))
-        first = [swap(w, "zh") for w in mine[:2]]
-        near_own = spread(jnp.stack(mine), "y", ny)
+        acts = spread(jnp.stack([acts, swap(acts, "zb")]), "za", na)
+
+        mine = jnp.concatenate([gate_weight.T, up_weight.T, down_weight])
+        cut = mine.shape[0] * 17 // 21
+        near = copies(mine, ny)
+        first, last = mine[:cut], mine[cut:]
+        near, first, acts = lax.optimization_barrier((near, first, acts))
+        first = swap(first, "zh")
+        near_own = lax.all_to_all(near, "y", 0, 0, tiled=True)
         acts = shifted(acts, "x", nx)
-        last = mine[2]
         acts, near_own, first, last = lax.optimization_barrier((acts, near_own, first, last))
 
         last = swap(last, "zh")
-        first_own = spread(jnp.stack(first), "y", ny)
+        first_own = spread(first, "y", ny)
         near_core = swap(near_own, "c")
         part, tok_far = near_layer(place, acts, (near_own, near_core))
         first_own, last, part = lax.optimization_barrier((first_own, last, part))
 
         first_core = swap(first_own, "c")
-        last_own = spread(last[None], "y", ny)
+        last_own = spread(last, "y", ny)
         last_core = swap(last_own, "c")
         weights = (near_own, near_core, first_own, first_core, last_own, last_core)
-        outs, grad = layer(place, part, tok_far, ia3_scale.reshape(1, -1), weights, nx, nl)
-
+        outs, grad = layer(place, part, tok_far, ia3_scale.reshape(1, -1), weights, nx, nb * na)
+
+        grad = grad + swap(grad, "zh")
         grad = grad + swap(grad, "c")
-        grad = total(shifted(grad, "y", ny))
-
         outs = lax.all_to_all(outs, "x", 0, 0, tiled=True)
         outs = total([outs[i] for i in range(nx)]).astype(BF16)
         outs, grad = lax.optimization_barrier((outs, grad))
-        scale_grad = (grad + swap(grad, "zh")).reshape(-1)
-        outs = lax.all_to_all(outs, "zl", 0, 0, tiled=True)
-        outs = total([outs[i] for i in range(nl)]).astype(BF16)
+        scale_grad = total(shifted(grad, "y", ny)).reshape(-1)
+        outs = outs.reshape((nb, na) + outs.shape[1:]).swapaxes(0, 1)
+        outs = lax.all_to_all(outs, "za", 0, 0, tiled=True)
+        outs = total([outs[i] for i in range(na)])
+        mine, theirs = [
+            lax.dynamic_index_in_dim(outs, jnp.bitwise_xor(place[3], k), 0, False) for k in range(2)
+        ]
+        outs = (mine + swap(theirs.astype(BF16), "zb").astype(F32)).astype(BF16)
         return outs[0].reshape(tokens.shape), outs[1].reshape(tokens.shape), scale_grad
 
     return per_device
 
 
 def solution(mesh):
-    shape = {"zh": 2, "y": 4, "c": 2, "x": 4, "zl": 8}
+    shape = {"zh": 2, "y": 4, "c": 2, "x": 4, "zb": 2, "za": 4}
     fine = Mesh(mesh.devices.reshape(tuple(shape.values())), tuple(shape))
     in_specs = (
         P(None, ROWS_AXES, COLS_AXES),

time: 245 us -> 230 us (0.939)
  blocking collectives: 58.1 us -> 12.8 us
  starting transfers between devices: 74.5 us -> 118 us
  waiting for transfers between devices: 80.6 us -> 71 us
  local copies, waits for them, and re-layouts: 12.6 us -> 8.9 us
    all_to_all x2 -> x1, blocking collectives: 58.1 us -> 12.8 us  [spread(): return lax.all_to_all(copies(block, size), axis, 0, 0, tiled=True)]
    ppermute x8 -> x9, waiting for transfers between devices: 52.5 us -> 16.7 us  [swap(): return lax.ppermute(block, axis, [(0, 1), (1, 0)])]
    ppermute x8 -> x9, starting transfers between devices: 35.5 us -> 64 us  [swap(): return lax.ppermute(block, axis, [(0, 1), (1, 0)])]
    ppermute x6, waiting for transfers between devices: 2.38 us -> 17.2 us  [shifted(): lax.ppermute(block, axis, [(i, (i + n) % size) for i in range(size)])]
    all_to_all x3 -> x4, starting transfers between devices: 14.7 us -> 28.7 us  [the longest x1 15.6 us: per_device(): outs = lax.all_to_all(outs, 'za', 0, 0, tiled=True)]
    all_to_all x3 -> x4, waiting for transfers between devices: 14.8 us -> 27.6 us  [the longest x2 23.2 us: spread(): return lax.all_to_all(copies(block, size), axis, 0, 0, tiled=True)]
    unnamed x24 -> x14, local copies, waits for them, and re-layouts: 7.65 us -> 2.49 us
  transfers between devices with their start and end apart: 18 -> 20, of which waited for: 10 -> 13; matrix products, arithmetic and copies ran while one was open for 1% -> 1% of each run, Pallas kernels for 2% -> 2%
where the time goes in v3:
time: 230 us; the launch traced here: 226 us
  starting transfers between devices  118 us (51%)
  waiting for transfers between devices  71 us (31%)
  blocking collectives  12.8 us (6%)
  Pallas kernels  12.7 us (6%)
  local copies, waits for them, and re-layouts  8.9 us (4%)
    ppermute x9, starting transfers between devices, swap(): return lax.ppermute(block, axis, [(0, 1), (1, 0)])  64 us
    all_to_all x2, waiting for transfers between devices, spread(): return lax.all_to_all(copies(block, size), axis, 0, 0, tiled=True)  23.2 us
    ppermute x6, starting transfers between devices, shifted(): lax.ppermute(block, axis, [(i, (i + n) % size) for i in range(size)])  20.6 us
    ppermute x6, waiting for transfers between devices, shifted(): lax.ppermute(block, axis, [(i, (i + n) % size) for i in range(size)])  17.2 us
    ppermute x9, waiting for transfers between devices, swap(): return lax.ppermute(block, axis, [(0, 1), (1, 0)])  16.7 us
    all_to_all x1, starting transfers between devices, per_device(): outs = lax.all_to_all(outs, 'za', 0, 0, tiled=True)  15.6 us
    all_to_all x1, blocking collectives, spread(): return lax.all_to_all(copies(block, size), axis, 0, 0, tiled=True)  12.8 us
    all_to_all x1, waiting for transfers between devices, per_device(): outs = lax.all_to_all(outs, 'x', 0, 0, tiled=True)  9.4 us
  transfers between devices with their start and end apart: 20, of which 13 were waited for; matrix products, arithmetic and copies ran while one was open for 1% of the time, Pallas kernels for 2%

profile of v3, /device:TPU:24, one launch (start us, length us, event | category | flops | bytes accessed | tf_op | source)
XLA Modules:
  0.0 225.8 jit_solution(9249777772437231143)
XLA Ops:
  0.7 0.9 fusion.3
  1.5 9.1 %collective-permute-start = (bf16[2,128,128]{2,1,0:T(8,128)(2,1)S(1)}, bf16[2,128,128]{2,1,0:T(8,128)(2,1)S(1)}, u32[]{:S(2)}, u32[]{:S(2)}) collective-permute-start(bf16[2,128,128]{2,1,0:T(8,128)(2,1)S(1)} %get-tuple-element.44), channel_id=1, source_target_pairs={{0,4},{4,0},{1,5},{5,1},{2,6},{6,2},{3,7},{7,3},{8,12},{12,8},{9,1... | collective-permute-start | bytes 196616 | tf_op jit(solution)/shard_map/ppermute | solution.py:30
  10.6 6.4 %collective-permute-done = bf16[2,128,128]{2,1,0:T(8,128)(2,1)S(1)} collective-permute-done((bf16[2,128,128]{2,1,0:T(8,128)(2,1)S(1)}, bf16[2,128,128]{2,1,0:T(8,128)(2,1)S(1)}, u32[]{:S(2)}, u32[]{:S(2)}) %collective-permute-start) | collective-permute-done | bytes 65568 | tf_op jit(solution)/shard_map/ppermute | solution.py:30
  17.1 0.9 broadcast_in_dim.9
  18.0 3.6 %all-to-all-start = ((bf16[4,2,2,128,128]{4,3,2,1,0:T(8,128)(2,1)}), bf16[4,2,2,128,128]{4,3,2,1,0:T(8,128)(2,1)S(1)}, u32[]{:S(2)}, u32[]{:S(2)}) async-start(bf16[4,2,2,128,128]{4,3,2,1,0:T(8,128)(2,1)} %broadcast_in_dim.9), calls=%async_computation | async-start | bytes 1048576 | tf_op jit(solution)/shard_map/all_to_all | solution.py:19
  21.7 14.4 %all-to-all-done.acts_0 = bf16[4,2,2,128,128]{4,3,2,1,0:T(8,128)(2,1)S(1)} async-done(((bf16[4,2,2,128,128]{4,3,2,1,0:T(8,128)(2,1)}), bf16[4,2,2,128,128]{4,3,2,1,0:T(8,128)(2,1)S(1)}, u32[]{:S(2)}, u32[]{:S(2)}) %all-to-all-start) | async-done | bytes 524320 | tf_op jit(solution)/shard_map/all_to_all | solution.py:19
  36.1 1.7 broadcast_in_dim.8
  37.9 4.8 %all-to-all-start.1 = ((bf16[4,1344,256]{2,1,0:T(8,128)(2,1)}), bf16[4,1344,256]{2,1,0:T(8,128)(2,1)}, u32[]{:S(2)}, u32[]{:S(2)}) async-start(bf16[4,1344,256]{2,1,0:T(8,128)(2,1)} %broadcast_in_dim.8), calls=%async_computation.1 | async-start | bytes 5505024 | tf_op jit(solution)/shard_map/all_to_all | solution.py:237
  42.6 13.8 %collective-permute-start.4 = (bf16[1088,256]{1,0:T(8,128)(2,1)S(1)}, bf16[1088,256]{1,0:T(8,128)(2,1)S(1)}, u32[]{:S(2)}, u32[]{:S(2)}) collective-permute-start(bf16[1088,256]{1,0:T(8,128)(2,1)S(1)} %slice.48), channel_id=1, source_target_pairs={{0,256},{256,0},{1,257},{257,1},{2,258},{258,2},{3,259},{259,3},{4... | collective-permute-start | bytes 1671176 | tf_op jit(solution)/shard_map/ppermute | solution.py:30
  56.4 3.4 %collective-permute-start.1 = (bf16[4,2,2,128,128]{4,3,2,1,0:T(8,128)(2,1)S(1)}, bf16[4,2,2,128,128]{4,3,2,1,0:T(8,128)(2,1)S(1)}, u32[]{:S(2)}, u32[]{:S(2)}) collective-permute-start(bf16[4,2,2,128,128]{4,3,2,1,0:T(8,128)(2,1)S(1)} %all-to-all-done.acts_0), channel_id=1, source_target_pairs={{0,8},{8,16},{16,24},{24,0},{1,9},{9,17},{17,25},{25,1},{2,10},{10... | collective-permute-start | bytes 1572872 | tf_op jit(solution)/shard_map/ppermute | solution.py:24
  59.8 4.6 %collective-permute-start.2 = (bf16[4,2,2,128,128]{4,3,2,1,0:T(8,128)(2,1)S(1)}, bf16[4,2,2,128,128]{4,3,2,1,0:T(8,128)(2,1)S(1)}, u32[]{:S(2)}, u32[]{:S(2)}) collective-permute-start(bf16[4,2,2,128,128]{4,3,2,1,0:T(8,128)(2,1)S(1)} %all-to-all-done.acts_0), channel_id=1, source_target_pairs={{0,16},{8,24},{16,0},{24,8},{1,17},{9,25},{17,1},{25,9},{2,18},{10... | collective-permute-start | bytes 1572872 | tf_op jit(solution)/shard_map/ppermute | solution.py:24
  64.5 3.3 %collective-permute-start.3 = (bf16[4,2,2,128,128]{4,3,2,1,0:T(8,128)(2,1)S(1)}, bf16[4,2,2,128,128]{4,3,2,1,0:T(8,128)(2,1)S(1)}, u32[]{:S(2)}, u32[]{:S(2)}) collective-permute-start(bf16[4,2,2,128,128]{4,3,2,1,0:T(8,128)(2,1)S(1)} %all-to-all-done.acts_0), channel_id=1, source_target_pairs={{0,24},{8,0},{16,8},{24,16},{1,25},{9,1},{17,9},{25,17},{2,26},{10... | collective-permute-start | bytes 1572872 | tf_op jit(solution)/shard_map/ppermute | solution.py:24
  67.8 0.7 slice.37
  68.5 4.9 %collective-permute-done.1.acts_1 = bf16[4,2,2,128,128]{4,3,2,1,0:T(8,128)(2,1)S(1)} collective-permute-done((bf16[4,2,2,128,128]{4,3,2,1,0:T(8,128)(2,1)S(1)}, bf16[4,2,2,128,128]{4,3,2,1,0:T(8,128)(2,1)S(1)}, u32[]{:S(2)}, u32[]{:S(2)}) %collective-permute-start.1) | collective-permute-done | bytes 524320 | tf_op jit(solution)/shard_map/ppermute | solution.py:24
  73.4 10.8 %collective-permute-done.2.acts_2 = bf16[4,2,2,128,128]{4,3,2,1,0:T(8,128)(2,1)S(1)} collective-permute-done((bf16[4,2,2,128,128]{4,3,2,1,0:T(8,128)(2,1)S(1)}, bf16[4,2,2,128,128]{4,3,2,1,0:T(8,128)(2,1)S(1)}, u32[]{:S(2)}, u32[]{:S(2)}) %collective-permute-start.2) | collective-permute-done | bytes 524320 | tf_op jit(solution)/shard_map/ppermute | solution.py:24
  84.2 1.6 collective-permute-done.3.acts_3
  85.7 2.0 collective-permute-done.4
  87.7 1.9 collective-permute-start.6
  89.6 1.6 broadcast_in_dim.10
  91.2 4.7 %all-to-all-start.2 = ((bf16[4,1088,256]{2,1,0:T(8,128)(2,1)}), bf16[4,1088,256]{2,1,0:T(8,128)(2,1)}, u32[]{:S(2)}, u32[]{:S(2)}) async-start(bf16[4,1088,256]{2,1,0:T(8,128)(2,1)} %broadcast_in_dim.10), calls=%async_computation.2 | async-start | bytes 4456448 | tf_op jit(solution)/shard_map/all_to_all | solution.py:19
  95.9 12.3 %collective-permute-start.5 = (bf16[256,256]{1,0:T(8,128)(2,1)}, bf16[256,256]{1,0:T(8,128)(2,1)S(1)}, u32[]{:S(2)}, u32[]{:S(2)}) collective-permute-start(bf16[256,256]{1,0:T(8,128)(2,1)} %slice.37), channel_id=1, source_target_pairs={{0,256},{256,0},{1,257},{257,1},{2,258},{258,2},{3,259},{259,3},{4... | collective-permute-start | bytes 393224 | tf_op jit(solution)/shard_map/ppermute | solution.py:30
  108.2 0.1 pad_add_fusion.place
  108.3 1.0 copy-done.1
  109.3 4.5 %shard_map.85 = (f32[3,128,448]{2,1,0:T(8,128)S(1)}, bf16[2,128,2048]{2,1,0:T(8,128)(2,1)S(1)}) custom-call(s32[4]{0:T(128)S(1)} %pad_add_fusion.place, bf16[4,2,2,128,128]{4,3,2,1,0:T(8,128)(2,1)S(1)} %all-to-all-done.acts_0, bf16[4,2,2,128,128]{4,3,2,1,0:T(8,128)(2,1)S(1)} %collective-permute-done.1.acts_1, ...), custom_call_target="tpu_custom_call" | custom-call | flops 704643072 | bytes 5505024 | tf_op jit(solution)/shard_map/pallas_call | solution.py:166
  113.8 8.8 %all-to-all-done.2.first_own = bf16[4,1088,256]{2,1,0:T(8,128)(2,1)} async-done(((bf16[4,1088,256]{2,1,0:T(8,128)(2,1)}), bf16[4,1088,256]{2,1,0:T(8,128)(2,1)}, u32[]{:S(2)}, u32[]{:S(2)}) %all-to-all-start.2) | async-done | bytes 2228256 | tf_op jit(solution)/shard_map/all_to_all | solution.py:19
  122.6 1.9 collective-permute-start.7
  124.5 12.8 %all_to_all.30.last_own = bf16[4,256,256]{2,1,0:T(8,128)(2,1)S(1)} all-to-all(bf16[4,256,256]{2,1,0:T(8,128)(2,1)S(1)} %broadcast_in_dim.11), channel_id=1, replica_groups=mesh['zh'=2,'y'=4,'c'=2,'x'=4,'zb'=2,'za'=4] {'y'}, dimensions={0} | all-to-all | bytes 1048576 | tf_op jit(solution)/shard_map/all_to_all | solution.py:19
  137.4 1.9 collective-permute-start.8
  139.3 1.9 collective-permute-done.8.last_core
  141.2 1.4 copy-done.3
  142.6 8.2 %shard_map.86 = (bf16[4,8,2,128,128]{4,3,2,1,0:T(8,128)(2,1)}, f32[1,448]{1,0:T(1,128)S(1)}) custom-call(s32[4]{0:T(128)S(1)} %pad_add_fusion.place, f32[3,128,448]{2,1,0:T(8,128)S(1)} %get-tuple-element.33.part, bf16[2,128,2048]{2,1,0:T(8,128)(2,1)S(1)} %get-tuple-element.34.tok_far, f32[1,448]{1,0:T(1,128)S(1)} %bitcast.29, ...), custom_call_target="tpu_custom_call" | custom-call | flops 2113929216 | bytes 11010048 | tf_op jit(solution)/shard_map/pallas_call | solution.py:191
  150.8 4.3 %all-to-all-start.4 = ((bf16[4,8,2,128,128]{4,3,2,1,0:T(8,128)(2,1)}), bf16[4,8,2,128,128]{4,3,2,1,0:T(8,128)(2,1)S(1)}, u32[]{:S(2)}, u32[]{:S(2)}) async-start(bf16[4,8,2,128,128]{4,3,2,1,0:T(8,128)(2,1)} %get-tuple-element.37), calls=%async_computation.4 | async-start | bytes 4194304 | tf_op jit(solution)/shard_map/all_to_all | solution.py:255
  155.1 12.3 %collective-permute-start.9 = (f32[1,448]{1,0:T(1,128)S(1)}, f32[1,448]{1,0:T(1,128)S(1)}, u32[]{:S(2)}, u32[]{:S(2)}) collective-permute-start(f32[1,448]{1,0:T(1,128)S(1)} %get-tuple-element.38), channel_id=1, source_target_pairs={{0,256},{256,0},{1,257},{257,1},{2,258},{258,2},{3,259},{259,3},{4... | collective-permute-start | bytes 5384 | tf_op jit(solution)/shard_map/ppermute | solution.py:30
  167.4 1.9 collective-permute-done.9
  169.3 1.9 collective-permute-start.10
  171.2 1.1 collective-permute-done.10
  172.3 9.4 %all-to-all-done.4 = bf16[4,8,2,128,128]{4,3,2,1,0:T(8,128)(2,1)S(1)} async-done(((bf16[4,8,2,128,128]{4,3,2,1,0:T(8,128)(2,1)}), bf16[4,8,2,128,128]{4,3,2,1,0:T(8,128)(2,1)S(1)}, u32[]{:S(2)}, u32[]{:S(2)}) %all-to-all-start.4) | async-done | bytes 2097184 | tf_op jit(solution)/shard_map/all_to_all | solution.py:255
  181.7 0.3 fusion
  182.1 0.8 copy.11
  182.9 15.6 %all-to-all-start.5 = ((bf16[4,2,2,128,128]{4,3,2,1,0:T(8,128)(2,1)}), bf16[4,2,2,128,128]{4,3,2,1,0:T(8,128)(2,1)S(1)}, u32[]{:S(2)}, u32[]{:S(2)}) async-start(bf16[4,2,2,128,128]{4,3,2,1,0:T(8,128)(2,1)} %bitcast.28), calls=%async_computation.5 | async-start | bytes 1048576 | tf_op jit(solution)/shard_map/all_to_all | solution.py:260
  198.5 4.0 %collective-permute-start.12 = (f32[1,448]{1,0:T(1,128)S(1)}, f32[1,448]{1,0:T(1,128)S(1)}, u32[]{:S(2)}, u32[]{:S(2)}) collective-permute-start(f32[1,448]{1,0:T(1,128)S(1)} %add.53), channel_id=1, source_target_pairs={{0,64},{64,128},{128,192},{192,0},{1,65},{65,129},{129,193},{193,1... | collective-permute-start | bytes 5384 | tf_op jit(solution)/shard_map/ppermute | solution.py:24
  202.5 2.1 collective-permute-start.13
  204.6 3.1 %collective-permute-start.14 = (f32[1,448]{1,0:T(1,128)S(1)}, f32[1,448]{1,0:T(1,128)S(1)}, u32[]{:S(2)}, u32[]{:S(2)}) collective-permute-start(f32[1,448]{1,0:T(1,128)S(1)} %add.53), channel_id=1, source_target_pairs={{0,192},{64,0},{128,64},{192,128},{1,193},{65,1},{129,65},{193,129... | collective-permute-start | bytes 5384 | tf_op jit(solution)/shard_map/ppermute | solution.py:24
  207.7 4.4 %all-to-all-done.5 = bf16[4,2,2,128,128]{4,3,2,1,0:T(8,128)(2,1)S(1)} async-done(((bf16[4,2,2,128,128]{4,3,2,1,0:T(8,128)(2,1)}), bf16[4,2,2,128,128]{4,3,2,1,0:T(8,128)(2,1)S(1)}, u32[]{:S(2)}, u32[]{:S(2)}) %all-to-all-start.5) | async-done | bytes 524320 | tf_op jit(solution)/shard_map/all_to_all | solution.py:260
  212.2 8.9 %collective-permute-start.11 = (bf16[2,128,128]{2,1,0:T(8,128)(2,1)S(1)}, bf16[2,128,128]{2,1,0:T(8,128)(2,1)S(1)}, u32[]{:S(2)}, u32[]{:S(2)}) collective-permute-start(bf16[2,128,128]{2,1,0:T(8,128)(2,1)S(1)} %fusion.2), channel_id=1, source_target_pairs={{0,4},{4,0},{1,5},{5,1},{2,6},{6,2},{3,7},{7,3},{8,12},{12,8},{9,1... | collective-permute-start | bytes 196616 | tf_op jit(solution)/shard_map/ppermute | solution.py:30
  221.2 0.6 add_add_fusion.1
  221.8 3.4 %collective-permute-done.11 = bf16[2,128,128]{2,1,0:T(8,128)(2,1)S(1)} collective-permute-done((bf16[2,128,128]{2,1,0:T(8,128)(2,1)S(1)}, bf16[2,128,128]{2,1,0:T(8,128)(2,1)S(1)}, u32[]{:S(2)}, u32[]{:S(2)}) %collective-permute-start.11) | collective-permute-done | bytes 65568 | tf_op jit(solution)/shard_map/ppermute | solution.py:30
  225.2 0.6 slice_bitcast_fusion
  (28 shorter events, 0.3 us)
Async XLA Ops:
  0.6 21.0 %copy-start.6 = (bf16[256,448]{0,1:T(8,128)(2,1)S(1)}, bf16[256,448]{0,1:T(8,128)(2,1)}, u32[]{:S(2)}) copy-start(bf16[256,448]{0,1:T(8,128)(2,1)} %param.7) | copy-start | bytes 688132
  0.6 21.0 %copy-start.5 = (bf16[256,448]{0,1:T(8,128)(2,1)S(1)}, bf16[256,448]{0,1:T(8,128)(2,1)}, u32[]{:S(2)}) copy-start(bf16[256,448]{0,1:T(8,128)(2,1)} %param.8) | copy-start | bytes 688132
  0.7 21.0 %copy-start.4 = (bf16[448,256]{1,0:T(8,128)(2,1)S(1)}, bf16[448,256]{1,0:T(8,128)(2,1)}, u32[]{:S(2)}) copy-start(bf16[448,256]{1,0:T(8,128)(2,1)} %param.9) | copy-start | bytes 688132
  1.5 15.5 %collective-permute-start = (bf16[2,128,128]{2,1,0:T(8,128)(2,1)S(1)}, bf16[2,128,128]{2,1,0:T(8,128)(2,1)S(1)}, u32[]{:S(2)}, u32[]{:S(2)}) collective-permute-start(bf16[2,128,128]{2,1,0:T(8,128)(2,1)S(1)} %get-tuple-element.44), channel_id=1, source_target_pairs={{0,4},{4,0},{1,5},{5,1},{2,6},{6,2},{3,7},{7,3},{8,12},{12,8},{9,1... | collective-permute-start | bytes 196616 | tf_op jit(solution)/shard_map/ppermute | solution.py:30
  18.0 18.2 %all-to-all-start = ((bf16[4,2,2,128,128]{4,3,2,1,0:T(8,128)(2,1)}), bf16[4,2,2,128,128]{4,3,2,1,0:T(8,128)(2,1)S(1)}, u32[]{:S(2)}, u32[]{:S(2)}) async-start(bf16[4,2,2,128,128]{4,3,2,1,0:T(8,128)(2,1)} %broadcast_in_dim.9), calls=%async_computation | async-start | bytes 1048576 | tf_op jit(solution)/shard_map/all_to_all | solution.py:19
  37.9 49.8 %all-to-all-start.1 = ((bf16[4,1344,256]{2,1,0:T(8,128)(2,1)}), bf16[4,1344,256]{2,1,0:T(8,128)(2,1)}, u32[]{:S(2)}, u32[]{:S(2)}) async-start(bf16[4,1344,256]{2,1,0:T(8,128)(2,1)} %broadcast_in_dim.8), calls=%async_computation.1 | async-start | bytes 5505024 | tf_op jit(solution)/shard_map/all_to_all | solution.py:237
  42.6 45.1 %collective-permute-start.4 = (bf16[1088,256]{1,0:T(8,128)(2,1)S(1)}, bf16[1088,256]{1,0:T(8,128)(2,1)S(1)}, u32[]{:S(2)}, u32[]{:S(2)}) collective-permute-start(bf16[1088,256]{1,0:T(8,128)(2,1)S(1)} %slice.48), channel_id=1, source_target_pairs={{0,256},{256,0},{1,257},{257,1},{2,258},{258,2},{3,259},{259,3},{4... | collective-permute-start | bytes 1671176 | tf_op jit(solution)/shard_map/ppermute | solution.py:30
  56.4 17.0 %collective-permute-start.1 = (bf16[4,2,2,128,128]{4,3,2,1,0:T(8,128)(2,1)S(1)}, bf16[4,2,2,128,128]{4,3,2,1,0:T(8,128)(2,1)S(1)}, u32[]{:S(2)}, u32[]{:S(2)}) collective-permute-start(bf16[4,2,2,128,128]{4,3,2,1,0:T(8,128)(2,1)S(1)} %all-to-all-done.acts_0), channel_id=1, source_target_pairs={{0,8},{8,16},{16,24},{24,0},{1,9},{9,17},{17,25},{25,1},{2,10},{10... | collective-permute-start | bytes 1572872 | tf_op jit(solution)/shard_map/ppermute | solution.py:24
  59.8 24.3 %collective-permute-start.2 = (bf16[4,2,2,128,128]{4,3,2,1,0:T(8,128)(2,1)S(1)}, bf16[4,2,2,128,128]{4,3,2,1,0:T(8,128)(2,1)S(1)}, u32[]{:S(2)}, u32[]{:S(2)}) collective-permute-start(bf16[4,2,2,128,128]{4,3,2,1,0:T(8,128)(2,1)S(1)} %all-to-all-done.acts_0), channel_id=1, source_target_pairs={{0,16},{8,24},{16,0},{24,8},{1,17},{9,25},{17,1},{25,9},{2,18},{10... | collective-permute-start | bytes 1572872 | tf_op jit(solution)/shard_map/ppermute | solution.py:24
  64.5 21.3 %collective-permute-start.3 = (bf16[4,2,2,128,128]{4,3,2,1,0:T(8,128)(2,1)S(1)}, bf16[4,2,2,128,128]{4,3,2,1,0:T(8,128)(2,1)S(1)}, u32[]{:S(2)}, u32[]{:S(2)}) collective-permute-start(bf16[4,2,2,128,128]{4,3,2,1,0:T(8,128)(2,1)S(1)} %all-to-all-done.acts_0), channel_id=1, source_target_pairs={{0,24},{8,0},{16,8},{24,16},{1,25},{9,1},{17,9},{25,17},{2,26},{10... | collective-permute-start | bytes 1572872 | tf_op jit(solution)/shard_map/ppermute | solution.py:24
  85.7 5.5 %copy-start = (bf16[4,2,2,128,128]{4,3,2,1,0:T(8,128)(2,1)}, bf16[4,2,2,128,128]{4,3,2,1,0:T(8,128)(2,1)S(1)}, u32[]{:S(2)}) copy-start(bf16[4,2,2,128,128]{4,3,2,1,0:T(8,128)(2,1)S(1)} %collective-permute-done.3.acts_3) | copy-start | bytes 1572868
  87.7 20.6 %collective-permute-start.6 = (bf16[4,1344,256]{2,1,0:T(8,128)(2,1)}, bf16[4,1344,256]{2,1,0:T(8,128)(2,1)}, u32[]{:S(2)}, u32[]{:S(2)}) collective-permute-start(bf16[4,1344,256]{2,1,0:T(8,128)(2,1)} %all-to-all-done.1.own.near_own), channel_id=1, source_target_pairs={{0,32},{32,0},{1,33},{33,1},{2,34},{34,2},{3,35},{35,3},{4,36},{36... | collective-permute-start | bytes 8257544 | tf_op jit(solution)/shard_map/ppermute | solution.py:30
  91.2 31.4 %all-to-all-start.2 = ((bf16[4,1088,256]{2,1,0:T(8,128)(2,1)}), bf16[4,1088,256]{2,1,0:T(8,128)(2,1)}, u32[]{:S(2)}, u32[]{:S(2)}) async-start(bf16[4,1088,256]{2,1,0:T(8,128)(2,1)} %broadcast_in_dim.10), calls=%async_computation.2 | async-start | bytes 4456448 | tf_op jit(solution)/shard_map/all_to_all | solution.py:19
  95.9 17.9 %collective-permute-start.5 = (bf16[256,256]{1,0:T(8,128)(2,1)}, bf16[256,256]{1,0:T(8,128)(2,1)S(1)}, u32[]{:S(2)}, u32[]{:S(2)}) collective-permute-start(bf16[256,256]{1,0:T(8,128)(2,1)} %slice.37), channel_id=1, source_target_pairs={{0,256},{256,0},{1,257},{257,1},{2,258},{258,2},{3,259},{259,3},{4... | collective-permute-start | bytes 393224 | tf_op jit(solution)/shard_map/ppermute | solution.py:30
  108.3 1.0 copy-start.1
  109.3 33.3 %copy-start.2 = (f32[448]{0:T(512)S(1)}, f32[448]{0:T(512)}, u32[]{:S(2)}) copy-start(f32[448]{0:T(512)} %param.10) | copy-start | bytes 5380
  122.6 18.6 %collective-permute-start.7 = (bf16[4,1088,256]{2,1,0:T(8,128)(2,1)}, bf16[4,1088,256]{2,1,0:T(8,128)(2,1)S(1)}, u32[]{:S(2)}, u32[]{:S(2)}) collective-permute-start(bf16[4,1088,256]{2,1,0:T(8,128)(2,1)} %all-to-all-done.2.first_own), channel_id=1, source_target_pairs={{0,32},{32,0},{1,33},{33,1},{2,34},{34,2},{3,35},{35,3},{4,36},{36... | collective-permute-start | bytes 6684680 | tf_op jit(solution)/shard_map/ppermute | solution.py:30
  137.4 3.8 %collective-permute-start.8 = (bf16[4,256,256]{2,1,0:T(8,128)(2,1)S(1)}, bf16[4,256,256]{2,1,0:T(8,128)(2,1)S(1)}, u32[]{:S(2)}, u32[]{:S(2)}) collective-permute-start(bf16[4,256,256]{2,1,0:T(8,128)(2,1)S(1)} %all_to_all.30.last_own), channel_id=1, source_target_pairs={{0,32},{32,0},{1,33},{33,1},{2,34},{34,2},{3,35},{35,3},{4,36},{36... | collective-permute-start | bytes 1572872 | tf_op jit(solution)/shard_map/ppermute | solution.py:30
  141.2 1.4 copy-start.3
  150.8 30.9 %all-to-all-start.4 = ((bf16[4,8,2,128,128]{4,3,2,1,0:T(8,128)(2,1)}), bf16[4,8,2,128,128]{4,3,2,1,0:T(8,128)(2,1)S(1)}, u32[]{:S(2)}, u32[]{:S(2)}) async-start(bf16[4,8,2,128,128]{4,3,2,1,0:T(8,128)(2,1)} %get-tuple-element.37), calls=%async_computation.4 | async-start | bytes 4194304 | tf_op jit(solution)/shard_map/all_to_all | solution.py:255
  155.1 14.2 %collective-permute-start.9 = (f32[1,448]{1,0:T(1,128)S(1)}, f32[1,448]{1,0:T(1,128)S(1)}, u32[]{:S(2)}, u32[]{:S(2)}) collective-permute-start(f32[1,448]{1,0:T(1,128)S(1)} %get-tuple-element.38), channel_id=1, source_target_pairs={{0,256},{256,0},{1,257},{257,1},{2,258},{258,2},{3,259},{259,3},{4... | collective-permute-start | bytes 5384 | tf_op jit(solution)/shard_map/ppermute | solution.py:30
  169.3 3.0 %collective-permute-start.10 = (f32[1,448]{1,0:T(1,128)S(1)}, f32[1,448]{1,0:T(1,128)S(1)}, u32[]{:S(2)}, u32[]{:S(2)}) collective-permute-start(f32[1,448]{1,0:T(1,128)S(1)} %add.52), channel_id=1, source_target_pairs={{0,32},{32,0},{1,33},{33,1},{2,34},{34,2},{3,35},{35,3},{4,36},{36... | collective-permute-start | bytes 5384 | tf_op jit(solution)/shard_map/ppermute | solution.py:30
  182.9 29.3 %all-to-all-start.5 = ((bf16[4,2,2,128,128]{4,3,2,1,0:T(8,128)(2,1)}), bf16[4,2,2,128,128]{4,3,2,1,0:T(8,128)(2,1)S(1)}, u32[]{:S(2)}, u32[]{:S(2)}) async-start(bf16[4,2,2,128,128]{4,3,2,1,0:T(8,128)(2,1)} %bitcast.28), calls=%async_computation.5 | async-start | bytes 1048576 | tf_op jit(solution)/shard_map/all_to_all | solution.py:260
  198.5 22.6 %collective-permute-start.12 = (f32[1,448]{1,0:T(1,128)S(1)}, f32[1,448]{1,0:T(1,128)S(1)}, u32[]{:S(2)}, u32[]{:S(2)}) collective-permute-start(f32[1,448]{1,0:T(1,128)S(1)} %add.53), channel_id=1, source_target_pairs={{0,64},{64,128},{128,192},{192,0},{1,65},{65,129},{129,193},{193,1... | collective-permute-start | bytes 5384 | tf_op jit(solution)/shard_map/ppermute | solution.py:24
  202.5 18.7 %collective-permute-start.13 = (f32[1,448]{1,0:T(1,128)S(1)}, f32[1,448]{1,0:T(1,128)S(1)}, u32[]{:S(2)}, u32[]{:S(2)}) collective-permute-start(f32[1,448]{1,0:T(1,128)S(1)} %add.53), channel_id=1, source_target_pairs={{0,128},{64,192},{128,0},{192,64},{1,129},{65,193},{129,1},{193,65... | collective-permute-start | bytes 5384 | tf_op jit(solution)/shard_map/ppermute | solution.py:24
  204.6 16.5 %collective-permute-start.14 = (f32[1,448]{1,0:T(1,128)S(1)}, f32[1,448]{1,0:T(1,128)S(1)}, u32[]{:S(2)}, u32[]{:S(2)}) collective-permute-start(f32[1,448]{1,0:T(1,128)S(1)} %add.53), channel_id=1, source_target_pairs={{0,192},{64,0},{128,64},{192,128},{1,193},{65,1},{129,65},{193,129... | collective-permute-start | bytes 5384 | tf_op jit(solution)/shard_map/ppermute | solution.py:24
  212.2 12.9 %collective-permute-start.11 = (bf16[2,128,128]{2,1,0:T(8,128)(2,1)S(1)}, bf16[2,128,128]{2,1,0:T(8,128)(2,1)S(1)}, u32[]{:S(2)}, u32[]{:S(2)}) collective-permute-start(bf16[2,128,128]{2,1,0:T(8,128)(2,1)S(1)} %fusion.2), channel_id=1, source_target_pairs={{0,4},{4,0},{1,5},{5,1},{2,6},{6,2},{3,7},{7,3},{8,12},{12,8},{9,1... | collective-permute-start | bytes 196616 | tf_op jit(solution)/shard_map/ppermute | solution.py:30

commit v4 on v3

--- a/solution.py
+++ b/solution.py
@@ -104,7 +104,8 @@
     far,
     sems,
 ):
-    nx, nl, _, rows, width = outs.shape
+    nx, na, nb, _, rows, width = outs.shape
+    nl = nb * na
     zh = place[0]
     far_copies = fetch(place, [(first_own, first_core), (last_own, last_core)], far, sems.at[1])
     near_copies = fetch(place, [(near_own, near_core)], near, sems.at[0])
@@ -145,8 +146,8 @@
                 x, zl = divmod(2 * n + side, nl)
                 x = half * (nx // 2) + x
                 piece = slice(side * width, (side + 1) * width)
-                outs[x, zl, 0] = mixed[:, piece].astype(BF16)
-                outs[x, zl, 1] = back_in[:, piece].astype(BF16)
+                outs[x, zl % na, zl // na, 0] = mixed[:, piece].astype(BF16)
+                outs[x, zl % na, zl // na, 1] = back_in[:, piece].astype(BF16)
 
 
 def whole():
@@ -183,15 +184,15 @@
     )(place, *acts, *weights)
 
 
-def layer(place, part, tok_far, scale, weights, nx, nl):
+def layer(place, part, tok_far, scale, weights, nx, nb, na):
     _, rows, half = tok_far.shape
     ny, height, _ = weights[0].shape
     hid = height // 3
-    width = 2 * half // (nx * nl)
+    width = 2 * half // (nx * nb * na)
     return pl.pallas_call(
         layer_kernel,
         out_shape=(
-            jax.ShapeDtypeStruct((nx, nl, 2, rows, width), BF16),
+            jax.ShapeDtypeStruct((nx, na, nb, 2, rows, width), BF16),
             jax.ShapeDtypeStruct((1, hid), F32),
         ),
         in_specs=[pl.BlockSpec(memory_space=pltpu.SMEM)] + [whole()] * 3 + [anywhere()] * 6,
@@ -226,12 +227,14 @@
         place = jnp.stack([lax.axis_index(a) for a in ("zh", "c", "x", "zb")])
 
         acts = jnp.stack([tokens.reshape(rows, width), cotangent.reshape(rows, width)])
-        acts = spread(jnp.stack([acts, swap(acts, "zb")]), "za", na)
-
         mine = jnp.concatenate([gate_weight.T, up_weight.T, down_weight])
         cut = mine.shape[0] * 17 // 21
         near = copies(mine, ny)
         first, last = mine[:cut], mine[cut:]
+        acts = jnp.stack([acts, swap(acts, "zb")])
+        acts, near, first = lax.optimization_barrier((acts, near, first))
+        acts = spread(acts, "za", na)
+
         near, first, acts = lax.optimization_barrier((near, first, acts))
         first = swap(first, "zh")
         near_own = lax.all_to_all(near, "y", 0, 0, tiled=True)
@@ -246,9 +249,10 @@
 
         first_core = swap(first_own, "c")
         last_own = spread(last, "y", ny)
+        last_own, first_core = lax.optimization_barrier((last_own, first_core))
         last_core = swap(last_own, "c")
         weights = (near_own, near_core, first_own, first_core, last_own, last_core)
-        outs, grad = layer(place, part, tok_far, ia3_scale.reshape(1, -1), weights, nx, nb * na)
+        outs, grad = layer(place, part, tok_far, ia3_scale.reshape(1, -1), weights, nx, nb, na)
 
         grad = grad + swap(grad, "zh")
         grad = grad + swap(grad, "c")
@@ -256,7 +260,6 @@
         outs = total([outs[i] for i in range(nx)]).astype(BF16)
         outs, grad = lax.optimization_barrier((outs, grad))
         scale_grad = total(shifted(grad, "y", ny)).reshape(-1)
-        outs = outs.reshape((nb, na) + outs.shape[1:]).swapaxes(0, 1)
         outs = lax.all_to_all(outs, "za", 0, 0, tiled=True)
         outs = total([outs[i] for i in range(na)])
         mine, theirs = [

time: 230 us -> 228 us (level)
  blocking collectives: 12.8 us -> 30.8 us
  starting transfers between devices: 118 us -> 103 us
  waiting for transfers between devices: 71 us -> 67.4 us
  local copies, waits for them, and re-layouts: 8.9 us -> 5.86 us
    all_to_all x1 -> x2, blocking collectives: 12.8 us -> 30.8 us  [spread(): return lax.all_to_all(copies(block, size), axis, 0, 0, tiled=True)]
    ppermute x9, starting transfers between devices: 64 us -> 49.1 us  [swap(): return lax.ppermute(block, axis, [(0, 1), (1, 0)])]
    all_to_all x2 -> x1, waiting for transfers between devices: 23.2 us -> 8.5 us  [spread(): return lax.all_to_all(copies(block, size), axis, 0, 0, tiled=True)]
    ppermute x9, waiting for transfers between devices: 16.7 us -> 28.2 us  [swap(): return lax.ppermute(block, axis, [(0, 1), (1, 0)])]
    all_to_all x2 -> x1, starting transfers between devices: 8.32 us -> 4.68 us  [spread(): return lax.all_to_all(copies(block, size), axis, 0, 0, tiled=True)]
    all_to_all x1, starting transfers between devices: 15.6 us -> 19.1 us  [per_device(): outs = lax.all_to_all(outs, 'za', 0, 0, tiled=True)]
  transfers between devices with their start and end apart: 20 -> 19, of which waited for: 13 -> 12; matrix products, arithmetic and copies ran while one was open for 1% -> 2% of each run, Pallas kernels for 2% -> 2%
where the time goes in v4:
time: 228 us; the launch traced here: 224 us
  starting transfers between devices  103 us (45%)
  waiting for transfers between devices  67.4 us (30%)
  blocking collectives  30.8 us (14%)
  Pallas kernels  12.7 us (6%)
  local copies, waits for them, and re-layouts  5.86 us (3%)
  other arithmetic  3.89 us (2%)
    ppermute x9, starting transfers between devices, swap(): return lax.ppermute(block, axis, [(0, 1), (1, 0)])  49.1 us
    all_to_all x2, blocking collectives, spread(): return lax.all_to_all(copies(block, size), axis, 0, 0, tiled=True)  30.8 us
    ppermute x9, waiting for transfers between devices, swap(): return lax.ppermute(block, axis, [(0, 1), (1, 0)])  28.2 us
    ppermute x6, starting transfers between devices, shifted(): lax.ppermute(block, axis, [(i, (i + n) % size) for i in range(size)])  20.6 us
    all_to_all x1, starting transfers between devices, per_device(): outs = lax.all_to_all(outs, 'za', 0, 0, tiled=True)  19.1 us
    ppermute x6, waiting for transfers between devices, shifted(): lax.ppermute(block, axis, [(i, (i + n) % size) for i in range(size)])  16.9 us
    all_to_all x1, waiting for transfers between devices, per_device(): outs = lax.all_to_all(outs, 'x', 0, 0, tiled=True)  9.4 us
    all_to_all x1, waiting for transfers between devices, spread(): return lax.all_to_all(copies(block, size), axis, 0, 0, tiled=True)  8.5 us
  transfers between devices with their start and end apart: 19, of which 12 were waited for; matrix products, arithmetic and copies ran while one was open for 2% of the time, Pallas kernels for 2%

profile of v4, /device:TPU:24, one launch (start us, length us, event | category | flops | bytes accessed | tf_op | source)
XLA Modules:
  0.0 224.0 jit_solution(14097568985565655793)
XLA Ops:
  0.6 0.8 fusion.3
  1.4 9.1 %collective-permute-start = (bf16[2,128,128]{2,1,0:T(8,128)(2,1)S(1)}, bf16[2,128,128]{2,1,0:T(8,128)(2,1)S(1)}, u32[]{:S(2)}, u32[]{:S(2)}) collective-permute-start(bf16[2,128,128]{2,1,0:T(8,128)(2,1)S(1)} %get-tuple-element.54), channel_id=1, source_target_pairs={{0,4},{4,0},{1,5},{5,1},{2,6},{6,2},{3,7},{7,3},{8,12},{12,8},{9,1... | collective-permute-start | bytes 196616 | tf_op jit(solution)/shard_map/ppermute | solution.py:30
  10.5 1.2 pad_maximum_fusion
  11.8 5.2 %collective-permute-done = bf16[2,128,128]{2,1,0:T(8,128)(2,1)S(1)} collective-permute-done((bf16[2,128,128]{2,1,0:T(8,128)(2,1)S(1)}, bf16[2,128,128]{2,1,0:T(8,128)(2,1)S(1)}, u32[]{:S(2)}, u32[]{:S(2)}) %collective-permute-start) | collective-permute-done | bytes 65568 | tf_op jit(solution)/shard_map/ppermute | solution.py:30
  17.0 1.7 broadcast_in_dim.8
  18.7 0.1 broadcast_in_dim.9
  18.8 18.0 %all_to_all.30.acts_0 = bf16[4,2,2,128,128]{4,3,2,1,0:T(8,128)(2,1)S(1)} all-to-all(bf16[4,2,2,128,128]{4,3,2,1,0:T(8,128)(2,1)S(1)} %broadcast_in_dim.9), channel_id=1, replica_groups=mesh['zh'=2,'y'=4,'c'=2,'x'=4,'zb'=2,'za'=4] {'za'}, dimensions={0} | all-to-all | bytes 1048576 | tf_op jit(solution)/shard_map/all_to_all | solution.py:19
  36.8 4.9 %all-to-all-start.1 = ((bf16[4,1344,256]{2,1,0:T(8,128)(2,1)}), bf16[4,1344,256]{2,1,0:T(8,128)(2,1)}, u32[]{:S(2)}, u32[]{:S(2)}) async-start(bf16[4,1344,256]{2,1,0:T(8,128)(2,1)} %broadcast_in_dim.8), calls=%async_computation.1 | async-start | bytes 5505024 | tf_op jit(solution)/shard_map/all_to_all | solution.py:240
  41.7 12.9 %collective-permute-start.4 = (bf16[1088,256]{1,0:T(8,128)(2,1)S(1)}, bf16[1088,256]{1,0:T(8,128)(2,1)S(1)}, u32[]{:S(2)}, u32[]{:S(2)}) collective-permute-start(bf16[1088,256]{1,0:T(8,128)(2,1)S(1)} %slice.48), channel_id=1, source_target_pairs={{0,256},{256,0},{1,257},{257,1},{2,258},{258,2},{3,259},{259,3},{4... | collective-permute-start | bytes 1671176 | tf_op jit(solution)/shard_map/ppermute | solution.py:30
  54.6 3.4 %collective-permute-start.1 = (bf16[4,2,2,128,128]{4,3,2,1,0:T(8,128)(2,1)S(1)}, bf16[4,2,2,128,128]{4,3,2,1,0:T(8,128)(2,1)S(1)}, u32[]{:S(2)}, u32[]{:S(2)}) collective-permute-start(bf16[4,2,2,128,128]{4,3,2,1,0:T(8,128)(2,1)S(1)} %all_to_all.30.acts_0), channel_id=1, source_target_pairs={{0,8},{8,16},{16,24},{24,0},{1,9},{9,17},{17,25},{25,1},{2,10},{10... | collective-permute-start | bytes 1572872 | tf_op jit(solution)/shard_map/ppermute | solution.py:24
  58.0 4.6 %collective-permute-start.2 = (bf16[4,2,2,128,128]{4,3,2,1,0:T(8,128)(2,1)S(1)}, bf16[4,2,2,128,128]{4,3,2,1,0:T(8,128)(2,1)S(1)}, u32[]{:S(2)}, u32[]{:S(2)}) collective-permute-start(bf16[4,2,2,128,128]{4,3,2,1,0:T(8,128)(2,1)S(1)} %all_to_all.30.acts_0), channel_id=1, source_target_pairs={{0,16},{8,24},{16,0},{24,8},{1,17},{9,25},{17,1},{25,9},{2,18},{10... | collective-permute-start | bytes 1572872 | tf_op jit(solution)/shard_map/ppermute | solution.py:24
  62.6 3.3 %collective-permute-start.3 = (bf16[4,2,2,128,128]{4,3,2,1,0:T(8,128)(2,1)S(1)}, bf16[4,2,2,128,128]{4,3,2,1,0:T(8,128)(2,1)S(1)}, u32[]{:S(2)}, u32[]{:S(2)}) collective-permute-start(bf16[4,2,2,128,128]{4,3,2,1,0:T(8,128)(2,1)S(1)} %all_to_all.30.acts_0), channel_id=1, source_target_pairs={{0,24},{8,0},{16,8},{24,16},{1,25},{9,1},{17,9},{25,17},{2,26},{10... | collective-permute-start | bytes 1572872 | tf_op jit(solution)/shard_map/ppermute | solution.py:24
  66.0 0.7 slice.37
  66.7 4.9 %collective-permute-done.1.acts_1 = bf16[4,2,2,128,128]{4,3,2,1,0:T(8,128)(2,1)S(1)} collective-permute-done((bf16[4,2,2,128,128]{4,3,2,1,0:T(8,128)(2,1)S(1)}, bf16[4,2,2,128,128]{4,3,2,1,0:T(8,128)(2,1)S(1)}, u32[]{:S(2)}, u32[]{:S(2)}) %collective-permute-start.1) | collective-permute-done | bytes 524320 | tf_op jit(solution)/shard_map/ppermute | solution.py:24
  71.6 10.4 %collective-permute-done.2.acts_2 = bf16[4,2,2,128,128]{4,3,2,1,0:T(8,128)(2,1)S(1)} collective-permute-done((bf16[4,2,2,128,128]{4,3,2,1,0:T(8,128)(2,1)S(1)}, bf16[4,2,2,128,128]{4,3,2,1,0:T(8,128)(2,1)S(1)}, u32[]{:S(2)}, u32[]{:S(2)}) %collective-permute-start.2) | collective-permute-done | bytes 524320 | tf_op jit(solution)/shard_map/ppermute | solution.py:24
  82.0 1.6 collective-permute-done.3.acts_3
  83.6 1.9 collective-permute-start.6
  85.5 1.6 broadcast_in_dim.10
  87.1 4.7 %all-to-all-start.2 = ((bf16[4,1088,256]{2,1,0:T(8,128)(2,1)}), bf16[4,1088,256]{2,1,0:T(8,128)(2,1)}, u32[]{:S(2)}, u32[]{:S(2)}) async-start(bf16[4,1088,256]{2,1,0:T(8,128)(2,1)} %broadcast_in_dim.10), calls=%async_computation.2 | async-start | bytes 4456448 | tf_op jit(solution)/shard_map/all_to_all | solution.py:19
  91.8 5.3 %collective-permute-start.5 = (bf16[256,256]{1,0:T(8,128)(2,1)}, bf16[256,256]{1,0:T(8,128)(2,1)S(1)}, u32[]{:S(2)}, u32[]{:S(2)}) collective-permute-start(bf16[256,256]{1,0:T(8,128)(2,1)} %slice.37), channel_id=1, source_target_pairs={{0,256},{256,0},{1,257},{257,1},{2,258},{258,2},{3,259},{259,3},{4... | collective-permute-start | bytes 393224 | tf_op jit(solution)/shard_map/ppermute | solution.py:30
  97.0 0.1 pad_add_fusion.place
  97.1 1.0 copy-done.1
  98.2 4.5 %shard_map.85 = (f32[3,128,448]{2,1,0:T(8,128)S(1)}, bf16[2,128,2048]{2,1,0:T(8,128)(2,1)S(1)}) custom-call(s32[4]{0:T(128)S(1)} %pad_add_fusion.place, bf16[4,2,2,128,128]{4,3,2,1,0:T(8,128)(2,1)S(1)} %all_to_all.30.acts_0, bf16[4,2,2,128,128]{4,3,2,1,0:T(8,128)(2,1)S(1)} %collective-permute-done.1.acts_1, ...), custom_call_target="tpu_custom_call" | custom-call | flops 704643072 | bytes 5505024 | tf_op jit(solution)/shard_map/pallas_call | solution.py:167
  102.7 7.3 %collective-permute-done.5 = bf16[256,256]{1,0:T(8,128)(2,1)S(1)} collective-permute-done((bf16[256,256]{1,0:T(8,128)(2,1)}, bf16[256,256]{1,0:T(8,128)(2,1)S(1)}, u32[]{:S(2)}, u32[]{:S(2)}) %collective-permute-start.5) | collective-permute-done | bytes 131104 | tf_op jit(solution)/shard_map/ppermute | solution.py:30
  110.0 8.5 %all-to-all-done.2.first_own = bf16[4,1088,256]{2,1,0:T(8,128)(2,1)} async-done(((bf16[4,1088,256]{2,1,0:T(8,128)(2,1)}), bf16[4,1088,256]{2,1,0:T(8,128)(2,1)}, u32[]{:S(2)}, u32[]{:S(2)}) %all-to-all-start.2) | async-done | bytes 2228256 | tf_op jit(solution)/shard_map/all_to_all | solution.py:19
  118.5 1.9 collective-permute-start.7
  120.4 12.8 %all_to_all.31.last_own = bf16[4,256,256]{2,1,0:T(8,128)(2,1)S(1)} all-to-all(bf16[4,256,256]{2,1,0:T(8,128)(2,1)S(1)} %broadcast_in_dim.11), channel_id=1, replica_groups=mesh['zh'=2,'y'=4,'c'=2,'x'=4,'zb'=2,'za'=4] {'y'}, dimensions={0} | all-to-all | bytes 1048576 | tf_op jit(solution)/shard_map/all_to_all | solution.py:19
  133.2 0.0 collective-permute-done.7.first_core
  133.2 1.9 collective-permute-start.8
  135.2 1.9 collective-permute-done.8.last_core
  137.0 8.2 %shard_map.86 = (bf16[4,4,2,2,128,128]{5,4,3,2,1,0:T(8,128)(2,1)}, f32[1,448]{1,0:T(1,128)S(1)}) custom-call(s32[4]{0:T(128)S(1)} %pad_add_fusion.place, f32[3,128,448]{2,1,0:T(8,128)S(1)} %get-tuple-element.41.part, bf16[2,128,2048]{2,1,0:T(8,128)(2,1)S(1)} %get-tuple-element.42.tok_far, f32[1,448]{1,0:T(1,128)S(1)} %bitcast.25, ...), custom_call_target="tpu_custom_call" | custom-call | flops 2113929216 | bytes 11010048 | tf_op jit(solution)/shard_map/pallas_call | solution.py:192
  145.2 4.3 %all-to-all-start.4 = ((bf16[4,4,2,2,128,128]{5,4,3,2,1,0:T(8,128)(2,1)}), bf16[4,4,2,2,128,128]{5,4,3,2,1,0:T(8,128)(2,1)S(1)}, u32[]{:S(2)}, u32[]{:S(2)}) async-start(bf16[4,4,2,2,128,128]{5,4,3,2,1,0:T(8,128)(2,1)} %get-tuple-element.47), calls=%async_computation.4 | async-start | bytes 4194304 | tf_op jit(solution)/shard_map/all_to_all | solution.py:259
  149.5 5.3 %collective-permute-start.9 = (f32[1,448]{1,0:T(1,128)S(1)}, f32[1,448]{1,0:T(1,128)S(1)}, u32[]{:S(2)}, u32[]{:S(2)}) collective-permute-start(f32[1,448]{1,0:T(1,128)S(1)} %get-tuple-element.48), channel_id=1, source_target_pairs={{0,256},{256,0},{1,257},{257,1},{2,258},{258,2},{3,259},{259,3},{4... | collective-permute-start | bytes 5384 | tf_op jit(solution)/shard_map/ppermute | solution.py:30
  154.8 8.9 %collective-permute-done.9 = f32[1,448]{1,0:T(1,128)S(1)} collective-permute-done((f32[1,448]{1,0:T(1,128)S(1)}, f32[1,448]{1,0:T(1,128)S(1)}, u32[]{:S(2)}, u32[]{:S(2)}) %collective-permute-start.9) | collective-permute-done | bytes 1824 | tf_op jit(solution)/shard_map/ppermute | solution.py:30
  163.7 1.9 collective-permute-start.10
  165.6 1.1 collective-permute-done.10
  166.8 9.4 %all-to-all-done.4 = bf16[4,4,2,2,128,128]{5,4,3,2,1,0:T(8,128)(2,1)S(1)} async-done(((bf16[4,4,2,2,128,128]{5,4,3,2,1,0:T(8,128)(2,1)}), bf16[4,4,2,2,128,128]{5,4,3,2,1,0:T(8,128)(2,1)S(1)}, u32[]{:S(2)}, u32[]{:S(2)}) %all-to-all-start.4) | async-done | bytes 2097184 | tf_op jit(solution)/shard_map/all_to_all | solution.py:259
  176.2 1.1 fusion
  177.3 19.1 %all-to-all-start.5 = ((bf16[4,2,2,128,128]{4,3,2,1,0:T(8,128)(2,1)}), bf16[4,2,2,128,128]{4,3,2,1,0:T(8,128)(2,1)S(1)}, u32[]{:S(2)}, u32[]{:S(2)}) async-start(bf16[4,2,2,128,128]{4,3,2,1,0:T(8,128)(2,1)} %fusion), calls=%async_computation.5 | async-start | bytes 1048576 | tf_op jit(solution)/shard_map/all_to_all | solution.py:263
  196.4 4.0 %collective-permute-start.12 = (f32[1,448]{1,0:T(1,128)S(1)}, f32[1,448]{1,0:T(1,128)S(1)}, u32[]{:S(2)}, u32[]{:S(2)}) collective-permute-start(f32[1,448]{1,0:T(1,128)S(1)} %add.53), channel_id=1, source_target_pairs={{0,64},{64,128},{128,192},{192,0},{1,65},{65,129},{129,193},{193,1... | collective-permute-start | bytes 5384 | tf_op jit(solution)/shard_map/ppermute | solution.py:24
  200.3 2.1 collective-permute-start.13
  202.5 3.1 %collective-permute-start.14 = (f32[1,448]{1,0:T(1,128)S(1)}, f32[1,448]{1,0:T(1,128)S(1)}, u32[]{:S(2)}, u32[]{:S(2)}) collective-permute-start(f32[1,448]{1,0:T(1,128)S(1)} %add.53), channel_id=1, source_target_pairs={{0,192},{64,0},{128,64},{192,128},{1,193},{65,1},{129,65},{193,129... | collective-permute-start | bytes 5384 | tf_op jit(solution)/shard_map/ppermute | solution.py:24
  205.6 4.4 %all-to-all-done.5 = bf16[4,2,2,128,128]{4,3,2,1,0:T(8,128)(2,1)S(1)} async-done(((bf16[4,2,2,128,128]{4,3,2,1,0:T(8,128)(2,1)}), bf16[4,2,2,128,128]{4,3,2,1,0:T(8,128)(2,1)S(1)}, u32[]{:S(2)}, u32[]{:S(2)}) %all-to-all-start.5) | async-done | bytes 524320 | tf_op jit(solution)/shard_map/all_to_all | solution.py:263
  210.0 0.1 add_add_fusion
  210.1 8.8 %collective-permute-start.11 = (bf16[2,128,128]{2,1,0:T(8,128)(2,1)S(1)}, bf16[2,128,128]{2,1,0:T(8,128)(2,1)S(1)}, u32[]{:S(2)}, u32[]{:S(2)}) collective-permute-start(bf16[2,128,128]{2,1,0:T(8,128)(2,1)S(1)} %fusion.2), channel_id=1, source_target_pairs={{0,4},{4,0},{1,5},{5,1},{2,6},{6,2},{3,7},{7,3},{8,12},{12,8},{9,1... | collective-permute-start | bytes 196616 | tf_op jit(solution)/shard_map/ppermute | solution.py:30
  219.0 0.6 add_add_fusion.1
  219.5 3.8 %collective-permute-done.11 = bf16[2,128,128]{2,1,0:T(8,128)(2,1)S(1)} collective-permute-done((bf16[2,128,128]{2,1,0:T(8,128)(2,1)S(1)}, bf16[2,128,128]{2,1,0:T(8,128)(2,1)S(1)}, u32[]{:S(2)}, u32[]{:S(2)}) %collective-permute-start.11) | collective-permute-done | bytes 65568 | tf_op jit(solution)/shard_map/ppermute | solution.py:30
  223.4 0.6 slice_bitcast_fusion
  (22 shorter events, 0.2 us)
Async XLA Ops:
  1.4 15.5 %collective-permute-start = (bf16[2,128,128]{2,1,0:T(8,128)(2,1)S(1)}, bf16[2,128,128]{2,1,0:T(8,128)(2,1)S(1)}, u32[]{:S(2)}, u32[]{:S(2)}) collective-permute-start(bf16[2,128,128]{2,1,0:T(8,128)(2,1)S(1)} %get-tuple-element.54), channel_id=1, source_target_pairs={{0,4},{4,0},{1,5},{5,1},{2,6},{6,2},{3,7},{7,3},{8,12},{12,8},{9,1... | collective-permute-start | bytes 196616 | tf_op jit(solution)/shard_map/ppermute | solution.py:30
  36.8 29.2 %copy-start.4 = (bf16[448,256]{1,0:T(8,128)(2,1)S(1)}, bf16[448,256]{1,0:T(8,128)(2,1)}, u32[]{:S(2)}) copy-start(bf16[448,256]{1,0:T(8,128)(2,1)} %param.9) | copy-start | bytes 688132
  36.8 46.8 %all-to-all-start.1 = ((bf16[4,1344,256]{2,1,0:T(8,128)(2,1)}), bf16[4,1344,256]{2,1,0:T(8,128)(2,1)}, u32[]{:S(2)}, u32[]{:S(2)}) async-start(bf16[4,1344,256]{2,1,0:T(8,128)(2,1)} %broadcast_in_dim.8), calls=%async_computation.1 | async-start | bytes 5505024 | tf_op jit(solution)/shard_map/all_to_all | solution.py:240
  41.7 41.9 %collective-permute-start.4 = (bf16[1088,256]{1,0:T(8,128)(2,1)S(1)}, bf16[1088,256]{1,0:T(8,128)(2,1)S(1)}, u32[]{:S(2)}, u32[]{:S(2)}) collective-permute-start(bf16[1088,256]{1,0:T(8,128)(2,1)S(1)} %slice.48), channel_id=1, source_target_pairs={{0,256},{256,0},{1,257},{257,1},{2,258},{258,2},{3,259},{259,3},{4... | collective-permute-start | bytes 1671176 | tf_op jit(solution)/shard_map/ppermute | solution.py:30
  54.6 17.0 %collective-permute-start.1 = (bf16[4,2,2,128,128]{4,3,2,1,0:T(8,128)(2,1)S(1)}, bf16[4,2,2,128,128]{4,3,2,1,0:T(8,128)(2,1)S(1)}, u32[]{:S(2)}, u32[]{:S(2)}) collective-permute-start(bf16[4,2,2,128,128]{4,3,2,1,0:T(8,128)(2,1)S(1)} %all_to_all.30.acts_0), channel_id=1, source_target_pairs={{0,8},{8,16},{16,24},{24,0},{1,9},{9,17},{17,25},{25,1},{2,10},{10... | collective-permute-start | bytes 1572872 | tf_op jit(solution)/shard_map/ppermute | solution.py:24
  58.0 24.0 %collective-permute-start.2 = (bf16[4,2,2,128,128]{4,3,2,1,0:T(8,128)(2,1)S(1)}, bf16[4,2,2,128,128]{4,3,2,1,0:T(8,128)(2,1)S(1)}, u32[]{:S(2)}, u32[]{:S(2)}) collective-permute-start(bf16[4,2,2,128,128]{4,3,2,1,0:T(8,128)(2,1)S(1)} %all_to_all.30.acts_0), channel_id=1, source_target_pairs={{0,16},{8,24},{16,0},{24,8},{1,17},{9,25},{17,1},{25,9},{2,18},{10... | collective-permute-start | bytes 1572872 | tf_op jit(solution)/shard_map/ppermute | solution.py:24
  62.6 20.9 %collective-permute-start.3 = (bf16[4,2,2,128,128]{4,3,2,1,0:T(8,128)(2,1)S(1)}, bf16[4,2,2,128,128]{4,3,2,1,0:T(8,128)(2,1)S(1)}, u32[]{:S(2)}, u32[]{:S(2)}) collective-permute-start(bf16[4,2,2,128,128]{4,3,2,1,0:T(8,128)(2,1)S(1)} %all_to_all.30.acts_0), channel_id=1, source_target_pairs={{0,24},{8,0},{16,8},{24,16},{1,25},{9,1},{17,9},{25,17},{2,26},{10... | collective-permute-start | bytes 1572872 | tf_op jit(solution)/shard_map/ppermute | solution.py:24
  83.5 3.5 %copy-start = (bf16[4,2,2,128,128]{4,3,2,1,0:T(8,128)(2,1)}, bf16[4,2,2,128,128]{4,3,2,1,0:T(8,128)(2,1)S(1)}, u32[]{:S(2)}) copy-start(bf16[4,2,2,128,128]{4,3,2,1,0:T(8,128)(2,1)S(1)} %collective-permute-done.3.acts_3) | copy-start | bytes 1572868
  83.6 13.6 %collective-permute-start.6 = (bf16[4,1344,256]{2,1,0:T(8,128)(2,1)}, bf16[4,1344,256]{2,1,0:T(8,128)(2,1)}, u32[]{:S(2)}, u32[]{:S(2)}) collective-permute-start(bf16[4,1344,256]{2,1,0:T(8,128)(2,1)} %all-to-all-done.1.own.near_own), channel_id=1, source_target_pairs={{0,32},{32,0},{1,33},{33,1},{2,34},{34,2},{3,35},{35,3},{4,36},{36... | collective-permute-start | bytes 8257544 | tf_op jit(solution)/shard_map/ppermute | solution.py:30
  87.1 31.4 %all-to-all-start.2 = ((bf16[4,1088,256]{2,1,0:T(8,128)(2,1)}), bf16[4,1088,256]{2,1,0:T(8,128)(2,1)}, u32[]{:S(2)}, u32[]{:S(2)}) async-start(bf16[4,1088,256]{2,1,0:T(8,128)(2,1)} %broadcast_in_dim.10), calls=%async_computation.2 | async-start | bytes 4456448 | tf_op jit(solution)/shard_map/all_to_all | solution.py:19
  91.8 18.2 %collective-permute-start.5 = (bf16[256,256]{1,0:T(8,128)(2,1)}, bf16[256,256]{1,0:T(8,128)(2,1)S(1)}, u32[]{:S(2)}, u32[]{:S(2)}) collective-permute-start(bf16[256,256]{1,0:T(8,128)(2,1)} %slice.37), channel_id=1, source_target_pairs={{0,256},{256,0},{1,257},{257,1},{2,258},{258,2},{3,259},{259,3},{4... | collective-permute-start | bytes 393224 | tf_op jit(solution)/shard_map/ppermute | solution.py:30
  97.1 1.0 copy-start.1
  98.2 38.9 %copy-start.2 = (f32[448]{0:T(512)S(1)}, f32[448]{0:T(512)}, u32[]{:S(2)}) copy-start(f32[448]{0:T(512)} %param.10) | copy-start | bytes 5380
  118.5 14.8 %collective-permute-start.7 = (bf16[4,1088,256]{2,1,0:T(8,128)(2,1)}, bf16[4,1088,256]{2,1,0:T(8,128)(2,1)S(1)}, u32[]{:S(2)}, u32[]{:S(2)}) collective-permute-start(bf16[4,1088,256]{2,1,0:T(8,128)(2,1)} %all-to-all-done.2.first_own), channel_id=1, source_target_pairs={{0,32},{32,0},{1,33},{33,1},{2,34},{34,2},{3,35},{35,3},{4,36},{36... | collective-permute-start | bytes 6684680 | tf_op jit(solution)/shard_map/ppermute | solution.py:30
  133.2 3.8 %copy-start.3 = (bf16[4,1088,256]{2,1,0:T(8,128)(2,1)}, bf16[4,1088,256]{2,1,0:T(8,128)(2,1)S(1)}, u32[]{:S(2)}) copy-start(bf16[4,1088,256]{2,1,0:T(8,128)(2,1)S(1)} %collective-permute-done.7.first_core) | copy-start | bytes 6684676
  133.2 3.8 %collective-permute-start.8 = (bf16[4,256,256]{2,1,0:T(8,128)(2,1)S(1)}, bf16[4,256,256]{2,1,0:T(8,128)(2,1)S(1)}, u32[]{:S(2)}, u32[]{:S(2)}) collective-permute-start(bf16[4,256,256]{2,1,0:T(8,128)(2,1)S(1)} %all_to_all.31.last_own), channel_id=1, source_target_pairs={{0,32},{32,0},{1,33},{33,1},{2,34},{34,2},{3,35},{35,3},{4,36},{36... | collective-permute-start | bytes 1572872 | tf_op jit(solution)/shard_map/ppermute | solution.py:30
  145.2 30.9 %all-to-all-start.4 = ((bf16[4,4,2,2,128,128]{5,4,3,2,1,0:T(8,128)(2,1)}), bf16[4,4,2,2,128,128]{5,4,3,2,1,0:T(8,128)(2,1)S(1)}, u32[]{:S(2)}, u32[]{:S(2)}) async-start(bf16[4,4,2,2,128,128]{5,4,3,2,1,0:T(8,128)(2,1)} %get-tuple-element.47), calls=%async_computation.4 | async-start | bytes 4194304 | tf_op jit(solution)/shard_map/all_to_all | solution.py:259
  149.5 14.2 %collective-permute-start.9 = (f32[1,448]{1,0:T(1,128)S(1)}, f32[1,448]{1,0:T(1,128)S(1)}, u32[]{:S(2)}, u32[]{:S(2)}) collective-permute-start(f32[1,448]{1,0:T(1,128)S(1)} %get-tuple-element.48), channel_id=1, source_target_pairs={{0,256},{256,0},{1,257},{257,1},{2,258},{258,2},{3,259},{259,3},{4... | collective-permute-start | bytes 5384 | tf_op jit(solution)/shard_map/ppermute | solution.py:30
  163.7 3.0 %collective-permute-start.10 = (f32[1,448]{1,0:T(1,128)S(1)}, f32[1,448]{1,0:T(1,128)S(1)}, u32[]{:S(2)}, u32[]{:S(2)}) collective-permute-start(f32[1,448]{1,0:T(1,128)S(1)} %add.52), channel_id=1, source_target_pairs={{0,32},{32,0},{1,33},{33,1},{2,34},{34,2},{3,35},{35,3},{4,36},{36... | collective-permute-start | bytes 5384 | tf_op jit(solution)/shard_map/ppermute | solution.py:30
  177.3 32.7 %all-to-all-start.5 = ((bf16[4,2,2,128,128]{4,3,2,1,0:T(8,128)(2,1)}), bf16[4,2,2,128,128]{4,3,2,1,0:T(8,128)(2,1)S(1)}, u32[]{:S(2)}, u32[]{:S(2)}) async-start(bf16[4,2,2,128,128]{4,3,2,1,0:T(8,128)(2,1)} %fusion), calls=%async_computation.5 | async-start | bytes 1048576 | tf_op jit(solution)/shard_map/all_to_all | solution.py:263
  196.4 22.6 %collective-permute-start.12 = (f32[1,448]{1,0:T(1,128)S(1)}, f32[1,448]{1,0:T(1,128)S(1)}, u32[]{:S(2)}, u32[]{:S(2)}) collective-permute-start(f32[1,448]{1,0:T(1,128)S(1)} %add.53), channel_id=1, source_target_pairs={{0,64},{64,128},{128,192},{192,0},{1,65},{65,129},{129,193},{193,1... | collective-permute-start | bytes 5384 | tf_op jit(solution)/shard_map/ppermute | solution.py:24
  200.3 18.6 %collective-permute-start.13 = (f32[1,448]{1,0:T(1,128)S(1)}, f32[1,448]{1,0:T(1,128)S(1)}, u32[]{:S(2)}, u32[]{:S(2)}) collective-permute-start(f32[1,448]{1,0:T(1,128)S(1)} %add.53), channel_id=1, source_target_pairs={{0,128},{64,192},{128,0},{192,64},{1,129},{65,193},{129,1},{193,65... | collective-permute-start | bytes 5384 | tf_op jit(solution)/shard_map/ppermute | solution.py:24
  202.5 16.5 %collective-permute-start.14 = (f32[1,448]{1,0:T(1,128)S(1)}, f32[1,448]{1,0:T(1,128)S(1)}, u32[]{:S(2)}, u32[]{:S(2)}) collective-permute-start(f32[1,448]{1,0:T(1,128)S(1)} %add.53), channel_id=1, source_target_pairs={{0,192},{64,0},{128,64},{192,128},{1,193},{65,1},{129,65},{193,129... | collective-permute-start | bytes 5384 | tf_op jit(solution)/shard_map/ppermute | solution.py:24
  210.1 13.3 %collective-permute-start.11 = (bf16[2,128,128]{2,1,0:T(8,128)(2,1)S(1)}, bf16[2,128,128]{2,1,0:T(8,128)(2,1)S(1)}, u32[]{:S(2)}, u32[]{:S(2)}) collective-permute-start(bf16[2,128,128]{2,1,0:T(8,128)(2,1)S(1)} %fusion.2), channel_id=1, source_target_pairs={{0,4},{4,0},{1,5},{5,1},{2,6},{6,2},{3,7},{7,3},{8,12},{12,8},{9,1... | collective-permute-start | bytes 196616 | tf_op jit(solution)/shard_map/ppermute | solution.py:30

commit v5 on v4

--- a/solution.py
+++ b/solution.py
@@ -43,7 +43,8 @@
             for k, ref in enumerate(pair):
                 core = jnp.bitwise_xor(place[1], k)
                 for y in range(ny):
-                    at = pl.multiple_of((y * 2 + core) * depth, depth)
+                    block = y if len(pair) == 1 else y * 2 + core
+                    at = pl.multiple_of(block * depth, depth)
                     copy = pltpu.make_async_copy(
                         ref.at[y, pl.ds(start, count)],
                         weights.at[m, pl.ds(first, count), pl.ds(at, depth)],
@@ -97,7 +98,8 @@
     tok_far,
     scale,
     near_own, near_core,
-    first_own, first_core, last_own, last_core,
+    first_own, first_core,
+    last,
     outs,
     grad,
     near,
@@ -107,7 +109,7 @@
     nx, na, nb, _, rows, width = outs.shape
     nl = nb * na
     zh = place[0]
-    far_copies = fetch(place, [(first_own, first_core), (last_own, last_core)], far, sems.at[1])
+    far_copies = fetch(place, [(first_own, first_core), (last,)], far, sems.at[1])
     near_copies = fetch(place, [(near_own, near_core)], near, sems.at[0])
 
     def times(t, m):
@@ -195,7 +197,7 @@
             jax.ShapeDtypeStruct((nx, na, nb, 2, rows, width), BF16),
             jax.ShapeDtypeStruct((1, hid), F32),
         ),
-        in_specs=[pl.BlockSpec(memory_space=pltpu.SMEM)] + [whole()] * 3 + [anywhere()] * 6,
+        in_specs=[pl.BlockSpec(memory_space=pltpu.SMEM)] + [whole()] * 3 + [anywhere()] * 5,
         out_specs=(whole(), whole()),
         scratch_shapes=[
             pltpu.VMEM((3, hid, half), BF16),
@@ -248,10 +250,8 @@
         first_own, last, part = lax.optimization_barrier((first_own, last, part))
 
         first_core = swap(first_own, "c")
-        last_own = spread(last, "y", ny)
-        last_own, first_core = lax.optimization_barrier((last_own, first_core))
-        last_core = swap(last_own, "c")
-        weights = (near_own, near_core, first_own, first_core, last_own, last_core)
+        last = spread(last, ("y", "c"), 2 * ny)
+        weights = (near_own, near_core, first_own, first_core, last)
         outs, grad = layer(place, part, tok_far, ia3_scale.reshape(1, -1), weights, nx, nb, na)
 
         grad = grad + swap(grad, "zh")

time: 228 us -> 228 us (level)
  blocking collectives: 30.8 us -> 36.5 us
  waiting for transfers between devices: 67.4 us -> 63.6 us
    all_to_all x2, blocking collectives: 30.8 us -> 36.5 us  [spread(): return lax.all_to_all(copies(block, size), axis, 0, 0, tiled=True)]
    ppermute x9 -> x8, waiting for transfers between devices: 28.2 us -> 25.8 us  [swap(): return lax.ppermute(block, axis, [(0, 1), (1, 0)])]
    ppermute x9 -> x8, starting transfers between devices: 49.1 us -> 47.2 us  [swap(): return lax.ppermute(block, axis, [(0, 1), (1, 0)])]
  transfers between devices with their start and end apart: 19 -> 18, of which waited for: 12 -> 11; matrix products, arithmetic and copies ran while one was open for 2% -> 2% of each run, Pallas kernels for 2% -> 2%
where the time goes in v5:
time: 228 us; the launch traced here: 226 us
  starting transfers between devices  101 us (44%)
  waiting for transfers between devices  63.6 us (28%)
  blocking collectives  36.5 us (16%)
  Pallas kernels  12.7 us (6%)
  local copies, waits for them, and re-layouts  7.36 us (3%)
  other arithmetic  3.91 us (2%)
    ppermute x8, starting transfers between devices, swap(): return lax.ppermute(block, axis, [(0, 1), (1, 0)])  47.2 us
    all_to_all x2, blocking collectives, spread(): return lax.all_to_all(copies(block, size), axis, 0, 0, tiled=True)  36.5 us
    ppermute x8, waiting for transfers between devices, swap(): return lax.ppermute(block, axis, [(0, 1), (1, 0)])  25.8 us
    ppermute x6, starting transfers between devices, shifted(): lax.ppermute(block, axis, [(i, (i + n) % size) for i in range(size)])  20.6 us
    all_to_all x1, starting transfers between devices, per_device(): outs = lax.all_to_all(outs, 'za', 0, 0, tiled=True)  19.1 us
    ppermute x6, waiting for transfers between devices, shifted(): lax.ppermute(block, axis, [(i, (i + n) % size) for i in range(size)])  16.9 us
    all_to_all x1, waiting for transfers between devices, per_device(): outs = lax.all_to_all(outs, 'x', 0, 0, tiled=True)  8.74 us
    all_to_all x1, waiting for transfers between devices, spread(): return lax.all_to_all(copies(block, size), axis, 0, 0, tiled=True)  8.52 us
  transfers between devices with their start and end apart: 18, of which 11 were waited for; matrix products, arithmetic and copies ran while one was open for 2% of the time, Pallas kernels for 2%

profile of v5, /device:TPU:24, one launch (start us, length us, event | category | flops | bytes accessed | tf_op | source)
XLA Modules:
  0.0 225.6 jit_solution(9947874145802724667)
XLA Ops:
  0.6 0.8 fusion.3
  1.4 9.1 %collective-permute-start = (bf16[2,128,128]{2,1,0:T(8,128)(2,1)S(1)}, bf16[2,128,128]{2,1,0:T(8,128)(2,1)S(1)}, u32[]{:S(2)}, u32[]{:S(2)}) collective-permute-start(bf16[2,128,128]{2,1,0:T(8,128)(2,1)S(1)} %get-tuple-element.50), channel_id=1, source_target_pairs={{0,4},{4,0},{1,5},{5,1},{2,6},{6,2},{3,7},{7,3},{8,12},{12,8},{9,1... | collective-permute-start | bytes 196616 | tf_op jit(solution)/shard_map/ppermute | solution.py:30
  10.5 1.2 pad_maximum_fusion
  11.8 5.2 %collective-permute-done = bf16[2,128,128]{2,1,0:T(8,128)(2,1)S(1)} collective-permute-done((bf16[2,128,128]{2,1,0:T(8,128)(2,1)S(1)}, bf16[2,128,128]{2,1,0:T(8,128)(2,1)S(1)}, u32[]{:S(2)}, u32[]{:S(2)}) %collective-permute-start) | collective-permute-done | bytes 65568 | tf_op jit(solution)/shard_map/ppermute | solution.py:30
  17.0 1.7 broadcast_in_dim.8
  18.7 0.1 broadcast_in_dim.9
  18.8 18.0 %all_to_all.30.acts_0 = bf16[4,2,2,128,128]{4,3,2,1,0:T(8,128)(2,1)S(1)} all-to-all(bf16[4,2,2,128,128]{4,3,2,1,0:T(8,128)(2,1)S(1)} %broadcast_in_dim.9), channel_id=1, replica_groups=mesh['zh'=2,'y'=4,'c'=2,'x'=4,'zb'=2,'za'=4] {'za'}, dimensions={0} | all-to-all | bytes 1048576 | tf_op jit(solution)/shard_map/all_to_all | solution.py:19
  36.8 4.9 %all-to-all-start.1 = ((bf16[4,1344,256]{2,1,0:T(8,128)(2,1)}), bf16[4,1344,256]{2,1,0:T(8,128)(2,1)}, u32[]{:S(2)}, u32[]{:S(2)}) async-start(bf16[4,1344,256]{2,1,0:T(8,128)(2,1)} %broadcast_in_dim.8), calls=%async_computation.1 | async-start | bytes 5505024 | tf_op jit(solution)/shard_map/all_to_all | solution.py:242
  41.7 12.9 %collective-permute-start.4 = (bf16[1088,256]{1,0:T(8,128)(2,1)S(1)}, bf16[1088,256]{1,0:T(8,128)(2,1)S(1)}, u32[]{:S(2)}, u32[]{:S(2)}) collective-permute-start(bf16[1088,256]{1,0:T(8,128)(2,1)S(1)} %slice.48), channel_id=1, source_target_pairs={{0,256},{256,0},{1,257},{257,1},{2,258},{258,2},{3,259},{259,3},{4... | collective-permute-start | bytes 1671176 | tf_op jit(solution)/shard_map/ppermute | solution.py:30
  54.6 3.4 %collective-permute-start.1 = (bf16[4,2,2,128,128]{4,3,2,1,0:T(8,128)(2,1)S(1)}, bf16[4,2,2,128,128]{4,3,2,1,0:T(8,128)(2,1)S(1)}, u32[]{:S(2)}, u32[]{:S(2)}) collective-permute-start(bf16[4,2,2,128,128]{4,3,2,1,0:T(8,128)(2,1)S(1)} %all_to_all.30.acts_0), channel_id=1, source_target_pairs={{0,8},{8,16},{16,24},{24,0},{1,9},{9,17},{17,25},{25,1},{2,10},{10... | collective-permute-start | bytes 1572872 | tf_op jit(solution)/shard_map/ppermute | solution.py:24
  58.0 4.6 %collective-permute-start.2 = (bf16[4,2,2,128,128]{4,3,2,1,0:T(8,128)(2,1)S(1)}, bf16[4,2,2,128,128]{4,3,2,1,0:T(8,128)(2,1)S(1)}, u32[]{:S(2)}, u32[]{:S(2)}) collective-permute-start(bf16[4,2,2,128,128]{4,3,2,1,0:T(8,128)(2,1)S(1)} %all_to_all.30.acts_0), channel_id=1, source_target_pairs={{0,16},{8,24},{16,0},{24,8},{1,17},{9,25},{17,1},{25,9},{2,18},{10... | collective-permute-start | bytes 1572872 | tf_op jit(solution)/shard_map/ppermute | solution.py:24
  62.7 3.3 %collective-permute-start.3 = (bf16[4,2,2,128,128]{4,3,2,1,0:T(8,128)(2,1)S(1)}, bf16[4,2,2,128,128]{4,3,2,1,0:T(8,128)(2,1)S(1)}, u32[]{:S(2)}, u32[]{:S(2)}) collective-permute-start(bf16[4,2,2,128,128]{4,3,2,1,0:T(8,128)(2,1)S(1)} %all_to_all.30.acts_0), channel_id=1, source_target_pairs={{0,24},{8,0},{16,8},{24,16},{1,25},{9,1},{17,9},{25,17},{2,26},{10... | collective-permute-start | bytes 1572872 | tf_op jit(solution)/shard_map/ppermute | solution.py:24
  66.0 0.7 slice.37
  66.7 4.9 %collective-permute-done.1.acts_1 = bf16[4,2,2,128,128]{4,3,2,1,0:T(8,128)(2,1)S(1)} collective-permute-done((bf16[4,2,2,128,128]{4,3,2,1,0:T(8,128)(2,1)S(1)}, bf16[4,2,2,128,128]{4,3,2,1,0:T(8,128)(2,1)S(1)}, u32[]{:S(2)}, u32[]{:S(2)}) %collective-permute-start.1) | collective-permute-done | bytes 524320 | tf_op jit(solution)/shard_map/ppermute | solution.py:24
  71.6 10.4 %collective-permute-done.2.acts_2 = bf16[4,2,2,128,128]{4,3,2,1,0:T(8,128)(2,1)S(1)} collective-permute-done((bf16[4,2,2,128,128]{4,3,2,1,0:T(8,128)(2,1)S(1)}, bf16[4,2,2,128,128]{4,3,2,1,0:T(8,128)(2,1)S(1)}, u32[]{:S(2)}, u32[]{:S(2)}) %collective-permute-start.2) | collective-permute-done | bytes 524320 | tf_op jit(solution)/shard_map/ppermute | solution.py:24
  82.0 1.6 collective-permute-done.3.acts_3
  83.6 1.9 collective-permute-start.6
  85.5 1.6 broadcast_in_dim.10
  87.1 4.7 %all-to-all-start.2 = ((bf16[4,1088,256]{2,1,0:T(8,128)(2,1)}), bf16[4,1088,256]{2,1,0:T(8,128)(2,1)}, u32[]{:S(2)}, u32[]{:S(2)}) async-start(bf16[4,1088,256]{2,1,0:T(8,128)(2,1)} %broadcast_in_dim.10), calls=%async_computation.2 | async-start | bytes 4456448 | tf_op jit(solution)/shard_map/all_to_all | solution.py:19
  91.8 5.3 %collective-permute-start.5 = (bf16[256,256]{1,0:T(8,128)(2,1)}, bf16[256,256]{1,0:T(8,128)(2,1)S(1)}, u32[]{:S(2)}, u32[]{:S(2)}) collective-permute-start(bf16[256,256]{1,0:T(8,128)(2,1)} %slice.37), channel_id=1, source_target_pairs={{0,256},{256,0},{1,257},{257,1},{2,258},{258,2},{3,259},{259,3},{4... | collective-permute-start | bytes 393224 | tf_op jit(solution)/shard_map/ppermute | solution.py:30
  97.1 0.1 pad_add_fusion.place
  97.2 1.0 copy-done.1
  98.2 4.5 %shard_map.85 = (f32[3,128,448]{2,1,0:T(8,128)S(1)}, bf16[2,128,2048]{2,1,0:T(8,128)(2,1)S(1)}) custom-call(s32[4]{0:T(128)S(1)} %pad_add_fusion.place, bf16[4,2,2,128,128]{4,3,2,1,0:T(8,128)(2,1)S(1)} %all_to_all.30.acts_0, bf16[4,2,2,128,128]{4,3,2,1,0:T(8,128)(2,1)S(1)} %collective-permute-done.1.acts_1, ...), custom_call_target="tpu_custom_call" | custom-call | flops 704643072 | bytes 5505024 | tf_op jit(solution)/shard_map/pallas_call | solution.py:169
  102.7 0.0 copy-start.2
  102.7 7.3 %collective-permute-done.5 = bf16[256,256]{1,0:T(8,128)(2,1)S(1)} collective-permute-done((bf16[256,256]{1,0:T(8,128)(2,1)}, bf16[256,256]{1,0:T(8,128)(2,1)S(1)}, u32[]{:S(2)}, u32[]{:S(2)}) %collective-permute-start.5) | collective-permute-done | bytes 131104 | tf_op jit(solution)/shard_map/ppermute | solution.py:30
  110.0 8.5 %all-to-all-done.2.first_own = bf16[4,1088,256]{2,1,0:T(8,128)(2,1)} async-done(((bf16[4,1088,256]{2,1,0:T(8,128)(2,1)}), bf16[4,1088,256]{2,1,0:T(8,128)(2,1)}, u32[]{:S(2)}, u32[]{:S(2)}) %all-to-all-start.2) | async-done | bytes 2228256 | tf_op jit(solution)/shard_map/all_to_all | solution.py:19
  118.5 1.9 collective-permute-start.7
  120.4 0.1 broadcast_in_dim.11
  120.5 18.5 %all_to_all.31.last = bf16[8,256,256]{2,1,0:T(8,128)(2,1)S(1)} all-to-all(bf16[8,256,256]{2,1,0:T(8,128)(2,1)S(1)} %broadcast_in_dim.11), channel_id=1, replica_groups=mesh['zh'=2,'y'=4,'c'=2,'x'=4,'zb'=2,'za'=4] {'y','c'}, dimensions={0} | all-to-all | bytes 2097152 | tf_op jit(solution)/shard_map/all_to_all | solution.py:19
  139.0 1.5 copy-done.3
  140.5 8.2 %shard_map.86 = (bf16[4,4,2,2,128,128]{5,4,3,2,1,0:T(8,128)(2,1)}, f32[1,448]{1,0:T(1,128)S(1)}) custom-call(s32[4]{0:T(128)S(1)} %pad_add_fusion.place, f32[3,128,448]{2,1,0:T(8,128)S(1)} %get-tuple-element.39.part, bf16[2,128,2048]{2,1,0:T(8,128)(2,1)S(1)} %get-tuple-element.40.tok_far, f32[1,448]{1,0:T(1,128)S(1)} %bitcast.25, ...), custom_call_target="tpu_custom_call" | custom-call | flops 2113929216 | bytes 11010048 | tf_op jit(solution)/shard_map/pallas_call | solution.py:194
  148.7 4.3 %all-to-all-start.4 = ((bf16[4,4,2,2,128,128]{5,4,3,2,1,0:T(8,128)(2,1)}), bf16[4,4,2,2,128,128]{5,4,3,2,1,0:T(8,128)(2,1)S(1)}, u32[]{:S(2)}, u32[]{:S(2)}) async-start(bf16[4,4,2,2,128,128]{5,4,3,2,1,0:T(8,128)(2,1)} %get-tuple-element.43), calls=%async_computation.4 | async-start | bytes 4194304 | tf_op jit(solution)/shard_map/all_to_all | solution.py:259
  153.0 5.3 %collective-permute-start.8 = (f32[1,448]{1,0:T(1,128)S(1)}, f32[1,448]{1,0:T(1,128)S(1)}, u32[]{:S(2)}, u32[]{:S(2)}) collective-permute-start(f32[1,448]{1,0:T(1,128)S(1)} %get-tuple-element.44), channel_id=1, source_target_pairs={{0,256},{256,0},{1,257},{257,1},{2,258},{258,2},{3,259},{259,3},{4... | collective-permute-start | bytes 5384 | tf_op jit(solution)/shard_map/ppermute | solution.py:30
  158.2 8.9 %collective-permute-done.8 = f32[1,448]{1,0:T(1,128)S(1)} collective-permute-done((f32[1,448]{1,0:T(1,128)S(1)}, f32[1,448]{1,0:T(1,128)S(1)}, u32[]{:S(2)}, u32[]{:S(2)}) %collective-permute-start.8) | collective-permute-done | bytes 1824 | tf_op jit(solution)/shard_map/ppermute | solution.py:30
  167.1 1.9 collective-permute-start.9
  169.1 1.1 collective-permute-done.9
  170.2 8.7 %all-to-all-done.4 = bf16[4,4,2,2,128,128]{5,4,3,2,1,0:T(8,128)(2,1)S(1)} async-done(((bf16[4,4,2,2,128,128]{5,4,3,2,1,0:T(8,128)(2,1)}), bf16[4,4,2,2,128,128]{5,4,3,2,1,0:T(8,128)(2,1)S(1)}, u32[]{:S(2)}, u32[]{:S(2)}) %all-to-all-start.4) | async-done | bytes 2097184 | tf_op jit(solution)/shard_map/all_to_all | solution.py:259
  178.9 1.1 fusion
  180.1 19.1 %all-to-all-start.5 = ((bf16[4,2,2,128,128]{4,3,2,1,0:T(8,128)(2,1)}), bf16[4,2,2,128,128]{4,3,2,1,0:T(8,128)(2,1)S(1)}, u32[]{:S(2)}, u32[]{:S(2)}) async-start(bf16[4,2,2,128,128]{4,3,2,1,0:T(8,128)(2,1)} %fusion), calls=%async_computation.5 | async-start | bytes 1048576 | tf_op jit(solution)/shard_map/all_to_all | solution.py:263
  199.1 4.0 %collective-permute-start.11 = (f32[1,448]{1,0:T(1,128)S(1)}, f32[1,448]{1,0:T(1,128)S(1)}, u32[]{:S(2)}, u32[]{:S(2)}) collective-permute-start(f32[1,448]{1,0:T(1,128)S(1)} %add.53), channel_id=1, source_target_pairs={{0,64},{64,128},{128,192},{192,0},{1,65},{65,129},{129,193},{193,1... | collective-permute-start | bytes 5384 | tf_op jit(solution)/shard_map/ppermute | solution.py:24
  203.1 2.1 collective-permute-start.12
  205.2 3.2 %collective-permute-start.13 = (f32[1,448]{1,0:T(1,128)S(1)}, f32[1,448]{1,0:T(1,128)S(1)}, u32[]{:S(2)}, u32[]{:S(2)}) collective-permute-start(f32[1,448]{1,0:T(1,128)S(1)} %add.53), channel_id=1, source_target_pairs={{0,192},{64,0},{128,64},{192,128},{1,193},{65,1},{129,65},{193,129... | collective-permute-start | bytes 5384 | tf_op jit(solution)/shard_map/ppermute | solution.py:24
  208.4 3.7 %all-to-all-done.5 = bf16[4,2,2,128,128]{4,3,2,1,0:T(8,128)(2,1)S(1)} async-done(((bf16[4,2,2,128,128]{4,3,2,1,0:T(8,128)(2,1)}), bf16[4,2,2,128,128]{4,3,2,1,0:T(8,128)(2,1)S(1)}, u32[]{:S(2)}, u32[]{:S(2)}) %all-to-all-start.5) | async-done | bytes 524320 | tf_op jit(solution)/shard_map/all_to_all | solution.py:263
  212.1 0.1 add_add_fusion
  212.1 8.8 %collective-permute-start.10 = (bf16[2,128,128]{2,1,0:T(8,128)(2,1)S(1)}, bf16[2,128,128]{2,1,0:T(8,128)(2,1)S(1)}, u32[]{:S(2)}, u32[]{:S(2)}) collective-permute-start(bf16[2,128,128]{2,1,0:T(8,128)(2,1)S(1)} %fusion.2), channel_id=1, source_target_pairs={{0,4},{4,0},{1,5},{5,1},{2,6},{6,2},{3,7},{7,3},{8,12},{12,8},{9,1... | collective-permute-start | bytes 196616 | tf_op jit(solution)/shard_map/ppermute | solution.py:30
  221.0 0.6 add_add_fusion.1
  221.6 3.3 %collective-permute-done.10 = bf16[2,128,128]{2,1,0:T(8,128)(2,1)S(1)} collective-permute-done((bf16[2,128,128]{2,1,0:T(8,128)(2,1)S(1)}, bf16[2,128,128]{2,1,0:T(8,128)(2,1)S(1)}, u32[]{:S(2)}, u32[]{:S(2)}) %collective-permute-start.10) | collective-permute-done | bytes 65568 | tf_op jit(solution)/shard_map/ppermute | solution.py:30
  224.9 0.6 slice_bitcast_fusion
  (20 shorter events, 0.1 us)
Async XLA Ops:
  1.4 15.5 %collective-permute-start = (bf16[2,128,128]{2,1,0:T(8,128)(2,1)S(1)}, bf16[2,128,128]{2,1,0:T(8,128)(2,1)S(1)}, u32[]{:S(2)}, u32[]{:S(2)}) collective-permute-start(bf16[2,128,128]{2,1,0:T(8,128)(2,1)S(1)} %get-tuple-element.50), channel_id=1, source_target_pairs={{0,4},{4,0},{1,5},{5,1},{2,6},{6,2},{3,7},{7,3},{8,12},{12,8},{9,1... | collective-permute-start | bytes 196616 | tf_op jit(solution)/shard_map/ppermute | solution.py:30
  36.8 29.2 %copy-start.4 = (bf16[448,256]{1,0:T(8,128)(2,1)S(1)}, bf16[448,256]{1,0:T(8,128)(2,1)}, u32[]{:S(2)}) copy-start(bf16[448,256]{1,0:T(8,128)(2,1)} %param.9) | copy-start | bytes 688132
  36.8 46.8 %all-to-all-start.1 = ((bf16[4,1344,256]{2,1,0:T(8,128)(2,1)}), bf16[4,1344,256]{2,1,0:T(8,128)(2,1)}, u32[]{:S(2)}, u32[]{:S(2)}) async-start(bf16[4,1344,256]{2,1,0:T(8,128)(2,1)} %broadcast_in_dim.8), calls=%async_computation.1 | async-start | bytes 5505024 | tf_op jit(solution)/shard_map/all_to_all | solution.py:242
  41.7 41.9 %collective-permute-start.4 = (bf16[1088,256]{1,0:T(8,128)(2,1)S(1)}, bf16[1088,256]{1,0:T(8,128)(2,1)S(1)}, u32[]{:S(2)}, u32[]{:S(2)}) collective-permute-start(bf16[1088,256]{1,0:T(8,128)(2,1)S(1)} %slice.48), channel_id=1, source_target_pairs={{0,256},{256,0},{1,257},{257,1},{2,258},{258,2},{3,259},{259,3},{4... | collective-permute-start | bytes 1671176 | tf_op jit(solution)/shard_map/ppermute | solution.py:30
  54.6 17.0 %collective-permute-start.1 = (bf16[4,2,2,128,128]{4,3,2,1,0:T(8,128)(2,1)S(1)}, bf16[4,2,2,128,128]{4,3,2,1,0:T(8,128)(2,1)S(1)}, u32[]{:S(2)}, u32[]{:S(2)}) collective-permute-start(bf16[4,2,2,128,128]{4,3,2,1,0:T(8,128)(2,1)S(1)} %all_to_all.30.acts_0), channel_id=1, source_target_pairs={{0,8},{8,16},{16,24},{24,0},{1,9},{9,17},{17,25},{25,1},{2,10},{10... | collective-permute-start | bytes 1572872 | tf_op jit(solution)/shard_map/ppermute | solution.py:24
  58.0 24.0 %collective-permute-start.2 = (bf16[4,2,2,128,128]{4,3,2,1,0:T(8,128)(2,1)S(1)}, bf16[4,2,2,128,128]{4,3,2,1,0:T(8,128)(2,1)S(1)}, u32[]{:S(2)}, u32[]{:S(2)}) collective-permute-start(bf16[4,2,2,128,128]{4,3,2,1,0:T(8,128)(2,1)S(1)} %all_to_all.30.acts_0), channel_id=1, source_target_pairs={{0,16},{8,24},{16,0},{24,8},{1,17},{9,25},{17,1},{25,9},{2,18},{10... | collective-permute-start | bytes 1572872 | tf_op jit(solution)/shard_map/ppermute | solution.py:24
  62.7 20.9 %collective-permute-start.3 = (bf16[4,2,2,128,128]{4,3,2,1,0:T(8,128)(2,1)S(1)}, bf16[4,2,2,128,128]{4,3,2,1,0:T(8,128)(2,1)S(1)}, u32[]{:S(2)}, u32[]{:S(2)}) collective-permute-start(bf16[4,2,2,128,128]{4,3,2,1,0:T(8,128)(2,1)S(1)} %all_to_all.30.acts_0), channel_id=1, source_target_pairs={{0,24},{8,0},{16,8},{24,16},{1,25},{9,1},{17,9},{25,17},{2,26},{10... | collective-permute-start | bytes 1572872 | tf_op jit(solution)/shard_map/ppermute | solution.py:24
  83.6 3.5 %copy-start = (bf16[4,2,2,128,128]{4,3,2,1,0:T(8,128)(2,1)}, bf16[4,2,2,128,128]{4,3,2,1,0:T(8,128)(2,1)S(1)}, u32[]{:S(2)}) copy-start(bf16[4,2,2,128,128]{4,3,2,1,0:T(8,128)(2,1)S(1)} %collective-permute-done.3.acts_3) | copy-start | bytes 1572868
  83.6 13.6 %collective-permute-start.6 = (bf16[4,1344,256]{2,1,0:T(8,128)(2,1)}, bf16[4,1344,256]{2,1,0:T(8,128)(2,1)}, u32[]{:S(2)}, u32[]{:S(2)}) collective-permute-start(bf16[4,1344,256]{2,1,0:T(8,128)(2,1)} %all-to-all-done.1.own.near_own), channel_id=1, source_target_pairs={{0,32},{32,0},{1,33},{33,1},{2,34},{34,2},{3,35},{35,3},{4,36},{36... | collective-permute-start | bytes 8257544 | tf_op jit(solution)/shard_map/ppermute | solution.py:30
  87.1 31.4 %all-to-all-start.2 = ((bf16[4,1088,256]{2,1,0:T(8,128)(2,1)}), bf16[4,1088,256]{2,1,0:T(8,128)(2,1)}, u32[]{:S(2)}, u32[]{:S(2)}) async-start(bf16[4,1088,256]{2,1,0:T(8,128)(2,1)} %broadcast_in_dim.10), calls=%async_computation.2 | async-start | bytes 4456448 | tf_op jit(solution)/shard_map/all_to_all | solution.py:19
  91.8 18.2 %collective-permute-start.5 = (bf16[256,256]{1,0:T(8,128)(2,1)}, bf16[256,256]{1,0:T(8,128)(2,1)S(1)}, u32[]{:S(2)}, u32[]{:S(2)}) collective-permute-start(bf16[256,256]{1,0:T(8,128)(2,1)} %slice.37), channel_id=1, source_target_pairs={{0,256},{256,0},{1,257},{257,1},{2,258},{258,2},{3,259},{259,3},{4... | collective-permute-start | bytes 393224 | tf_op jit(solution)/shard_map/ppermute | solution.py:30
  97.2 1.0 copy-start.1
  102.7 37.8 %copy-start.2 = (f32[448]{0:T(512)S(1)}, f32[448]{0:T(512)}, u32[]{:S(2)}) copy-start(f32[448]{0:T(512)} %param.10) | copy-start | bytes 5380
  118.5 20.5 %collective-permute-start.7 = (bf16[4,1088,256]{2,1,0:T(8,128)(2,1)}, bf16[4,1088,256]{2,1,0:T(8,128)(2,1)S(1)}, u32[]{:S(2)}, u32[]{:S(2)}) collective-permute-start(bf16[4,1088,256]{2,1,0:T(8,128)(2,1)} %all-to-all-done.2.first_own), channel_id=1, source_target_pairs={{0,32},{32,0},{1,33},{33,1},{2,34},{34,2},{3,35},{35,3},{4,36},{36... | collective-permute-start | bytes 6684680 | tf_op jit(solution)/shard_map/ppermute | solution.py:30
  139.0 1.5 copy-start.3
  148.7 30.3 %all-to-all-start.4 = ((bf16[4,4,2,2,128,128]{5,4,3,2,1,0:T(8,128)(2,1)}), bf16[4,4,2,2,128,128]{5,4,3,2,1,0:T(8,128)(2,1)S(1)}, u32[]{:S(2)}, u32[]{:S(2)}) async-start(bf16[4,4,2,2,128,128]{5,4,3,2,1,0:T(8,128)(2,1)} %get-tuple-element.43), calls=%async_computation.4 | async-start | bytes 4194304 | tf_op jit(solution)/shard_map/all_to_all | solution.py:259
  153.0 14.2 %collective-permute-start.8 = (f32[1,448]{1,0:T(1,128)S(1)}, f32[1,448]{1,0:T(1,128)S(1)}, u32[]{:S(2)}, u32[]{:S(2)}) collective-permute-start(f32[1,448]{1,0:T(1,128)S(1)} %get-tuple-element.44), channel_id=1, source_target_pairs={{0,256},{256,0},{1,257},{257,1},{2,258},{258,2},{3,259},{259,3},{4... | collective-permute-start | bytes 5384 | tf_op jit(solution)/shard_map/ppermute | solution.py:30
  167.1 3.0 %collective-permute-start.9 = (f32[1,448]{1,0:T(1,128)S(1)}, f32[1,448]{1,0:T(1,128)S(1)}, u32[]{:S(2)}, u32[]{:S(2)}) collective-permute-start(f32[1,448]{1,0:T(1,128)S(1)} %add.52), channel_id=1, source_target_pairs={{0,32},{32,0},{1,33},{33,1},{2,34},{34,2},{3,35},{35,3},{4,36},{36... | collective-permute-start | bytes 5384 | tf_op jit(solution)/shard_map/ppermute | solution.py:30
  180.1 32.0 %all-to-all-start.5 = ((bf16[4,2,2,128,128]{4,3,2,1,0:T(8,128)(2,1)}), bf16[4,2,2,128,128]{4,3,2,1,0:T(8,128)(2,1)S(1)}, u32[]{:S(2)}, u32[]{:S(2)}) async-start(bf16[4,2,2,128,128]{4,3,2,1,0:T(8,128)(2,1)} %fusion), calls=%async_computation.5 | async-start | bytes 1048576 | tf_op jit(solution)/shard_map/all_to_all | solution.py:263
  199.1 21.8 %collective-permute-start.11 = (f32[1,448]{1,0:T(1,128)S(1)}, f32[1,448]{1,0:T(1,128)S(1)}, u32[]{:S(2)}, u32[]{:S(2)}) collective-permute-start(f32[1,448]{1,0:T(1,128)S(1)} %add.53), channel_id=1, source_target_pairs={{0,64},{64,128},{128,192},{192,0},{1,65},{65,129},{129,193},{193,1... | collective-permute-start | bytes 5384 | tf_op jit(solution)/shard_map/ppermute | solution.py:24
  203.1 17.9 %collective-permute-start.12 = (f32[1,448]{1,0:T(1,128)S(1)}, f32[1,448]{1,0:T(1,128)S(1)}, u32[]{:S(2)}, u32[]{:S(2)}) collective-permute-start(f32[1,448]{1,0:T(1,128)S(1)} %add.53), channel_id=1, source_target_pairs={{0,128},{64,192},{128,0},{192,64},{1,129},{65,193},{129,1},{193,65... | collective-permute-start | bytes 5384 | tf_op jit(solution)/shard_map/ppermute | solution.py:24
  205.2 15.8 %collective-permute-start.13 = (f32[1,448]{1,0:T(1,128)S(1)}, f32[1,448]{1,0:T(1,128)S(1)}, u32[]{:S(2)}, u32[]{:S(2)}) collective-permute-start(f32[1,448]{1,0:T(1,128)S(1)} %add.53), channel_id=1, source_target_pairs={{0,192},{64,0},{128,64},{192,128},{1,193},{65,1},{129,65},{193,129... | collective-permute-start | bytes 5384 | tf_op jit(solution)/shard_map/ppermute | solution.py:24
  212.1 12.8 %collective-permute-start.10 = (bf16[2,128,128]{2,1,0:T(8,128)(2,1)S(1)}, bf16[2,128,128]{2,1,0:T(8,128)(2,1)S(1)}, u32[]{:S(2)}, u32[]{:S(2)}) collective-permute-start(bf16[2,128,128]{2,1,0:T(8,128)(2,1)S(1)} %fusion.2), channel_id=1, source_target_pairs={{0,4},{4,0},{1,5},{5,1},{2,6},{6,2},{3,7},{7,3},{8,12},{12,8},{9,1... | collective-permute-start | bytes 196616 | tf_op jit(solution)/shard_map/ppermute | solution.py:30
